TPU v7x, 512 devices: a whole 4x8x8 slice. The times are simulated.
512 devices in a mesh: row: 32 (over z, x), col: 16 (over y, core).
Axes of the slice: x: 4, y: 8, z: 8, core: 2. Of those that a mesh axis runs over, the one named last changes fastest.
Arguments:
- tokens: bfloat16 [512, 12288], P('row', 'col'), may hold values from -6 to 6
- weight_in: bfloat16 [12288, 24576], P('col', 'row'), may hold values from -0.0546875 to 0.0546875
- bias_in: float32 [24576], P('row'), may hold values from -3 to 3
- weight_out: bfloat16 [24576, 12288], P('row', 'col'), may hold values from -0.0390625 to 0.0390625
- out_grad: bfloat16 [512, 12288], P('row', 'col'), may hold values from -3 to 3
Outputs:
- grad_tokens: bfloat16 [512, 12288], P('row', 'col')
- grad_weight_in: bfloat16 [12288, 24576], P('col', 'row')
- grad_weight_out: bfloat16 [24576, 12288], P('row', 'col')
- grad_bias: float32 [24576], P('row')
All inputs are finite; a program needn't handle non-finite values.
Results may differ from a plain program's by a relative error of at most 0.0049.
Values may be sent and summed in bfloat16 or wider, within the bound.
A program may use at most 64 MiB of HBM per device.

v0:
```python
import jax
import jax.numpy as jnp
from jax import lax
from jax.sharding import PartitionSpec as P

SQRT_HALF = 0.7071067811865476
INV_ROOT_TWO_PI = 0.3989422804014327


def gelu_value(preact):
    return preact * 0.5 * (1.0 + lax.erf(preact * SQRT_HALF))


def gelu_slope(preact):
    return 0.5 * (1.0 + lax.erf(preact * SQRT_HALF)) + preact * INV_ROOT_TWO_PI * jnp.exp(
        -0.5 * preact * preact
    )


def body(tokens, weight_in, bias_in, weight_out, out_grad):
    features, upstream = (
        lax.all_gather(tokens, "row", axis=0, tiled=True),
        lax.all_gather(out_grad, "row", axis=0, tiled=True),
    )
    preact = (
        lax.psum_scatter(
            jnp.dot(features, weight_in, preferred_element_type=jnp.float32),
            "col",
            scatter_dimension=0,
            tiled=True,
        )
        + bias_in[None, :]
    )
    grad_act = lax.psum_scatter(
        lax.dot_general(
            upstream, weight_out, (((1,), (1,)), ((), ())), preferred_element_type=jnp.float32
        ),
        "col",
        scatter_dimension=0,
        tiled=True,
    )
    activated = gelu_value(preact).astype(jnp.bfloat16)
    grad_preact = (grad_act * gelu_slope(preact)).astype(jnp.bfloat16)
    act_piece = lax.all_gather(activated, "col", axis=0, tiled=True)
    grad_piece = lax.all_gather(grad_preact, "col", axis=0, tiled=True)
    grad_first = lax.dot_general(
        features, grad_piece, (((0,), (0,)), ((), ())), preferred_element_type=jnp.float32
    )
    grad_second = lax.dot_general(
        act_piece, upstream, (((0,), (0,)), ((), ())), preferred_element_type=jnp.float32
    )
    grad_shift = jnp.sum(grad_piece.astype(jnp.float32), axis=0)
    row_terms = lax.dot_general(
        grad_piece, weight_in, (((1,), (1,)), ((), ())), preferred_element_type=jnp.float32
    )
    input_terms = row_terms
    running = (grad_first, grad_second, grad_shift, input_terms)
    grad_first, grad_second, grad_shift, input_terms = running
    grad_tokens = lax.psum_scatter(input_terms, "row", scatter_dimension=0, tiled=True).astype(
        jnp.bfloat16
    )
    return (
        grad_tokens,
        grad_first.astype(jnp.bfloat16),
        grad_second.astype(jnp.bfloat16),
        grad_shift,
    )


def solution(mesh):
    in_specs = (P("row", "col"), P("col", "row"), P("row"), P("row", "col"), P("row", "col"))
    out_specs = (P("row", "col"), P("col", "row"), P("row", "col"), P("row"))
    return jax.shard_map(body, mesh=mesh, in_specs=in_specs, out_specs=out_specs, check_vma=False)
```

profile of v0, /device:TPU:1, one launch (start us, length us, event | category | flops | bytes accessed | tf_op | source)
XLA Modules:
  0.0 432.8 jit_solution(10738048960079003994)
XLA Ops:
  7.2 0.0 copy-start
  7.2 0.0 reduce-scatter.4.cloned.1.call-start
  7.2 44.7 %all_gather.12 = bf16[512,768]{1,0:T(8,128)(2,1)S(1)} all-gather(bf16[16,768]{1,0:T(8,128)(2,1)} %param.9), channel_id=1, replica_groups=mesh['row'=32,'col'=16] {'row'}, dimensions={0}, use_global_device_ids=true | all-gather | bytes 811008 | tf_op jit(solution)/shard_map/all_gather | solution.py:23
  51.9 0.0 copy-start.1
  51.9 0.9 copy-done.1
  52.8 3.2 fusion.6
  56.0 0.0 copy-start.4
  56.0 0.0 reduce-scatter.4.cloned.1.call-update
  56.0 0.0 reduce-scatter.6.cloned.1.call-start
  56.1 0.7 copy-done.4
  56.8 38.0 %all_gather.13 = bf16[512,768]{1,0:T(8,128)(2,1)S(1)} all-gather(bf16[16,768]{1,0:T(8,128)(2,1)S(1)} %copy-done.4), channel_id=1, replica_groups=mesh['row'=32,'col'=16] {'row'}, dimensions={0}, use_global_device_ids=true | all-gather | bytes 811008 | tf_op jit(solution)/shard_map/all_gather | solution.py:22
  94.8 0.0 copy-start.3
  94.8 0.9 copy-done.3
  95.7 0.0 copy-done
  95.7 1.9 fusion.7
  97.6 0.0 copy-start.5
  97.6 0.0 reduce-scatter.6.cloned.1.call-update
  97.6 0.0 reduce-scatter.8.cloned.1.call-start
  97.7 26.9 %reduce-scatter.4.cloned.1.call-done = f32[32,768]{1,0:T(8,128)} async-done(((f32[512,768]{1,0:T(8,128)}), f32[32,768]{1,0:T(8,128)}) %reduce-scatter.4.cloned.1.call-update) | async-done | bytes 98320 | tf_op jit(solution)/shard_map/reduce_scatter | solution.py:34
  124.6 62.3 %reduce-scatter.6.cloned.1.call-done = f32[32,768]{1,0:T(8,128)} async-done(((f32[512,768]{1,0:T(8,128)}), f32[32,768]{1,0:T(8,128)}) %reduce-scatter.6.cloned.1.call-update) | async-done | bytes 98320 | tf_op jit(solution)/shard_map/reduce_scatter | solution.py:26
  186.8 0.0 copy-done.5
  186.8 1.0 multiply_convert_fusion
  187.8 18.9 %all_gather.14 = bf16[512,768]{1,0:T(8,128)(2,1)S(1)} all-gather(bf16[32,768]{1,0:T(8,128)(2,1)S(1)} %get-tuple-element.9), channel_id=1, replica_groups=mesh['row'=32,'col'=16] {'col'}, dimensions={0}, use_global_device_ids=true | all-gather | bytes 835584 | tf_op jit(solution)/shard_map/all_gather | solution.py:45
  206.8 2.0 fusion.8
  208.7 0.0 reduce-scatter.8.cloned.1.call-update
  208.8 1.9 fusion
  210.7 1.5 copy.9
  212.2 0.0 copy-start.2
  212.2 0.7 convert_reduce_fusion
  212.9 17.9 %all_gather.15 = bf16[512,768]{1,0:T(8,128)(2,1)S(1)} all-gather(bf16[32,768]{1,0:T(8,128)(2,1)S(1)} %get-tuple-element.8), channel_id=1, replica_groups=mesh['row'=32,'col'=16] {'col'}, dimensions={0}, use_global_device_ids=true | all-gather | bytes 835584 | tf_op jit(solution)/shard_map/all_gather | solution.py:44
  230.8 0.0 copy-done.2
  230.9 1.8 convolution_convert_fusion
  232.7 192.2 %reduce-scatter.8.cloned.1.call-done = f32[16,768]{1,0:T(8,128)} async-done(((f32[512,768]{1,0:T(8,128)}), f32[16,768]{1,0:T(8,128)}) %reduce-scatter.8.cloned.1.call-update) | async-done | bytes 49168 | tf_op jit(solution)/shard_map/reduce_scatter | solution.py:59
  424.9 1.4 convert_element_type.22
Async XLA Ops:
  7.2 88.5 %copy-start = (bf16[768,768]{1,0:T(8,128)(2,1)S(1)}, bf16[768,768]{1,0:T(8,128)(2,1)}, u32[]{:S(2)}) copy-start(bf16[768,768]{1,0:T(8,128)(2,1)} %param.6) | copy-start | bytes 3538948
  7.2 117.4 %reduce-scatter.4.cloned.1.call-start = ((), (), s32[]{:S(2)}) async-start(), calls=%async_computation.3 | async-start | bytes 1671168 | tf_op jit(solution)/shard_map/reduce_scatter | solution.py:34
  51.9 0.9 copy-start.1
  56.0 0.7 copy-start.4
  56.0 130.8 %reduce-scatter.6.cloned.1.call-start = ((), (), s32[]{:S(2)}) async-start(), calls=%async_computation.4 | async-start | bytes 1671168 | tf_op jit(solution)/shard_map/reduce_scatter | solution.py:26
  94.8 0.9 copy-start.3
  97.6 89.3 %copy-start.5 = (f32[768]{0:T(1024)S(1)}, f32[768]{0:T(1024)}, u32[]{:S(2)}) copy-start(f32[768]{0:T(1024)} %param.7) | copy-start | bytes 9220
  97.6 327.2 %reduce-scatter.8.cloned.1.call-start = ((), (), s32[]{:S(2)}) async-start(), calls=%async_computation.5 | async-start | bytes 1622016 | tf_op jit(solution)/shard_map/reduce_scatter | solution.py:59
  212.2 18.7 %copy-start.2 = (bf16[512,768]{1,0:T(8,128)(2,1)S(1)}, bf16[512,768]{1,0:T(8,128)(2,1)}, u32[]{:S(2)}) copy-start(bf16[512,768]{1,0:T(8,128)(2,1)} %copy-done.1) | copy-start | bytes 2359300
Sparse Core Ops, SparseCore 0:
  56.2 68.3 reduce-scatter.3
  127.6 59.1 reduce-scatter.5
  208.9 215.9 reduce-scatter.7
where the time goes:
time: 438 us; the launch traced here: 433 us
  waiting for transfers between devices  281 us (64%)
  blocking collectives  120 us (27%)
  between operations  13.8 us (3%)
  matrix products  10.9 us (2%)
    reduce_scatter x1, waiting for transfers between devices, body(): lax.psum_scatter(input_terms, 'row', scatter_dimension=0, tiled=True)  192 us
    reduce_scatter x1, waiting for transfers between devices, body(): lax.psum_scatter(jnp.dot(features, weight_in, preferred_element_type=jnp....  62.3 us
    all_gather x1, blocking collectives, body(): lax.all_gather(out_grad, 'row', axis=0, tiled=True)  44.7 us
    all_gather x1, blocking collectives, body(): lax.all_gather(tokens, 'row', axis=0, tiled=True)  38 us
    reduce_scatter x1, waiting for transfers between devices, body(): lax.psum_scatter(lax.dot_general(upstream, weight_out, (((1,), (1,)), (()...  26.9 us
    all_gather x1, blocking collectives, body(): grad_piece = lax.all_gather(grad_preact, 'col', axis=0, tiled=True)  18.9 us
    all_gather x1, blocking collectives, body(): act_piece = lax.all_gather(activated, 'col', axis=0, tiled=True)  17.9 us
  transfers between devices with their start and end apart: 3, of which 3 were waited for; matrix products, arithmetic and copies ran while one was open for 2% of the time, Pallas kernels for 0%

commit v1 on v0

v1 whole, which is shorter than its diff:
```python
import functools

import jax
import jax.numpy as jnp
from jax import lax
from jax.experimental import pallas as pl
from jax.experimental.pallas import tpu as pltpu
from jax.sharding import PartitionSpec as P

SQRT_HALF = 0.7071067811865476
INV_ROOT_TWO_PI = 0.3989422804014327
X = 4
N_SEMS = 192
BF16, F32 = jnp.bfloat16, jnp.float32
MESH = pl.DeviceIdType.MESH


def gelu_value(preact):
    return preact * 0.5 * (1.0 + lax.erf(preact * SQRT_HALF))


def gelu_slope(preact):
    return 0.5 * (1.0 + lax.erf(preact * SQRT_HALF)) + preact * INV_ROOT_TWO_PI * jnp.exp(
        -0.5 * preact * preact
    )


def around(n):
    out = [0]
    for d in range(1, n // 2):
        out += [d, -d]
    return out + [n // 2]


def copy_out(a, b, c, d, a_out, b_out, c_out, d_out, sems):
    copies = [
        pltpu.make_async_copy(src, dst, sems.at[i])
        for i, (src, dst) in enumerate(((b, b_out), (c, c_out)))
    ]
    for copy in copies:
        copy.start()
    a_out[...] = a[...]
    d_out[...] = jnp.sum(d[...], axis=0)
    for copy in copies:
        copy.wait()


def kernel(
    nz,
    ny,
    tokens,
    weight_in,
    bias_in,
    weight_out,
    out_grad,
    grad_tokens,
    grad_weight_in,
    grad_weight_out,
    grad_bias,
    tok_all,
    og_all,
    w_in,
    w_out,
    part,
    pair_out,
    pair_in,
    ring_out,
    ring_in,
    act_all,
    gp_all,
    g_full,
    g_send,
    lx_in,
    lz_sum,
    lz_out,
    lz_in,
    rz_out,
    rz_in,
    rx_sum,
    rx_in,
    gwi,
    gwo,
    send_sems,
    recv_sems,
    local_sems,
):
    nx = X
    rows, feat = tokens.shape
    hid = w_in.shape[1]
    cut = lx_in.shape[-1]
    total = nz * nx * rows
    piece = total // (2 * ny)
    hz, hy = nz // 2, ny // 2
    row, col = lax.axis_index("row"), lax.axis_index("col")
    z, x = lax.div(row, nx), lax.rem(row, nx)
    y, c = lax.div(col, 2), lax.rem(col, 2)

    def yn(d):
        return lax.rem(y + (ny + d), ny)

    def to_z(d):
        return (lax.rem(z + (nz + d), nz) * nx + x, col)

    def to_x(d):
        return (z * nx + lax.rem(x + d, nx), col)

    def to_y(d):
        return (row, yn(d) * 2 + c)

    partner = (row, y * 2 + (1 - c))
    pending = []

    def send(src, dst, device):
        i = len(pending)
        copy = pltpu.make_async_remote_copy(
            src_ref=src,
            dst_ref=dst,
            send_sem=send_sems.at[i],
            recv_sem=recv_sems.at[i],
            device_id=device,
            device_id_type=MESH,
        )
        copy.start()
        pending.append(copy)
        return copy

    def local(src, dst, i):
        copy = pltpu.make_async_copy(src, dst, local_sems.at[i])
        copy.start()
        return copy

    left, right = pl.ds(0, cut), pl.ds(cut, feat - cut)
    slot = {d: i for i, d in enumerate(around(nz))}
    slot[-hz] = slot[hz]
    near = 2 * min(hz, 3) - 1

    def direct(h, side):
        out = []
        for d in (2, 1):
            if d < h:
                out += [d, -d]
            elif d == h:
                out.append(d * side)
        return out

    def relayed(h, side):
        return [(sgn, d) for sgn in (1, -1) for d in (3, 4) if d < h or (d == h and sgn == side)]

    own_tok = local(tokens, tok_all.at[0, 0], 0)
    own_og = local(out_grad, og_all.at[0, 0], 1)
    load_in = local(weight_in, w_in, 2)
    load_out = local(weight_out, w_out, 3)

    barrier = pltpu.get_barrier_semaphore()
    friends = [to_x(j) for j in range(1, nx)] + [partner]
    for d in (1, -1, 2, -2):
        friends += [to_z(d)] * (abs(d) <= hz) + [to_y(d)] * (abs(d) <= hy)
    for device in friends:
        pl.semaphore_signal(barrier, inc=1, device_id=device, device_id_type=MESH)
    pl.semaphore_wait(barrier, len(friends))

    sources = ((tokens, tok_all), (out_grad, og_all))
    sides = (1, -1)
    rx, lz, lx, rz = ({} for _ in range(4))

    for a, (src, buf) in enumerate(sources):
        for j in range(1, nx):
            rx[a, j] = send(src.at[:, right], buf.at[0, nx - j, :, right], to_x(j))
        for d in direct(hz, sides[a]):
            lz[a, d] = send(src.at[:, left], buf.at[slot[-d], 0, :, left], to_z(d))
    own_tok.wait()
    own_og.wait()
    for a, (_, buf) in enumerate(sources):
        for j in range(1, nx):
            rx[a, j].wait_recv()
        for d in direct(hz, sides[a]):
            rz[a, d] = send(buf.at[0, :, :, right], buf.at[slot[-d], :, :, right], to_z(d))
    for a, (_, buf) in enumerate(sources):
        for sgn, d in relayed(hz, sides[a]):
            if d == 3:
                lz[a, 2 * sgn].wait_recv()
            lz[a, d * sgn] = send(
                buf.at[slot[-2 * sgn], 0, :, left], buf.at[slot[-d * sgn], 0, :, left], to_z((d - 2) * sgn)
            )
        for d in direct(hz, sides[a]):
            if not (hz > 2 and abs(d) == 2):
                lz[a, d].wait_recv()
        for j in range(1, nx):
            lx[a, 0, j] = send(buf.at[0:near, 0, :, left], buf.at[0:near, nx - j, :, left], to_x(j))
    for a, (_, buf) in enumerate(sources):
        for sgn, d in relayed(hz, sides[a]):
            if d == 3:
                rz[a, 2 * sgn].wait_recv()
            rz[a, d * sgn] = send(
                buf.at[slot[-2 * sgn], :, :, right], buf.at[slot[-d * sgn], :, :, right], to_z((d - 2) * sgn)
            )
    for a, (_, buf) in enumerate(sources):
        for sgn, d in relayed(hz, sides[a]):
            lz[a, d * sgn].wait_recv()
        if near < nz:
            for j in range(1, nx):
                lx[a, 1, j] = send(
                    buf.at[near:nz, 0, :, left], buf.at[near:nz, nx - j, :, left], to_x(j)
                )

    def gathered(a):
        for d in direct(hz, sides[a]):
            if not (hz > 2 and abs(d) == 2):
                rz[a, d].wait_recv()
        for sgn, d in relayed(hz, sides[a]):
            rz[a, d * sgn].wait_recv()
        for key, copy in lx.items():
            if key[0] == a:
                copy.wait_recv()

    def product(a, core):
        buf = sources[a][1]
        rows_of = buf[pl.ds(core * hz, hz)].reshape(total // 2, feat)
        if a == 0:
            out = jnp.dot(rows_of, w_in[...], preferred_element_type=F32)
        else:
            out = lax.dot_general(
                rows_of, w_out[...], (((1,), (1,)), ((), ())), preferred_element_type=F32
            )
        return out.reshape(ny, piece, hid)

    def order(a):
        out = [d * sgn for sgn, d in relayed(hy, sides[a])]
        one = [d for d in direct(hy, sides[a]) if abs(d) == 1]
        two = [d for d in direct(hy, sides[a]) if abs(d) == 2]
        return out + one + two + [0]

    pair, ring = {}, {}

    def to_partner(a):
        pair_out[a] = product(a, 1 - c)
        for o in order(a):
            pair[a, o] = send(pair_out.at[a, yn(o)], pair_in.at[a, yn(o)], partner)

    def keep(a):
        part[a] = product(a, c)

    def chip_sum(a, o):
        pair[a, o].wait_recv()
        return part[a, yn(o)] + pair_in[a, yn(o)]

    def ring_send(a, k, value, d):
        i = len([key for key in ring if key[0] == a])
        ring_out[a, i] = value.astype(BF16)
        ring[a, k] = (send(ring_out.at[a, i], ring_in.at[a, i], to_y(d)), i)

    def ring_got(a, k):
        copy, i = ring[a, k]
        copy.wait_recv()
        return ring_in[a, i].astype(F32)

    def ring_first(a):
        for sgn, d in relayed(hy, sides[a]):
            ring_send(a, d * sgn, chip_sum(a, d * sgn), (d - 2) * sgn)
        for d in direct(hy, sides[a]):
            if abs(d) == 1:
                ring_send(a, d, chip_sum(a, d), d)

    def ring_second(a):
        for d in direct(hy, sides[a]):
            if abs(d) == 2:
                value = chip_sum(a, d)
                for sgn, far in relayed(hy, sides[a]):
                    if sgn * d > 0:
                        value = value + ring_got(a, far * sgn)
                ring_send(a, d, value, d)

    def ring_end(a):
        value = chip_sum(a, 0)
        for d in reversed(direct(hy, sides[a])):
            value = value + ring_got(a, d)
        return value

    load_in.wait()
    gathered(0)
    to_partner(0)
    keep(0)
    gathered(1)
    load_out.wait()
    to_partner(1)
    ring_first(0)
    keep(1)
    ring_first(1)
    ring_second(0)
    ring_second(1)
    preact = ring_end(0) + bias_in[...][None, :]
    act_all[c, y] = gelu_value(preact).astype(BF16)

    spread, shared = {}, {}

    def share(buf, k, o):
        block = buf.at[c, yn(o)]
        shared[k, o] = send(block, block, partner)

    def spread_first(buf, k):
        for d in direct(hy, sides[k]):
            block = buf.at[c, y]
            spread[k, d] = send(block, block, to_y(d))
        share(buf, k, 0)

    def spread_second(buf, k):
        relays = relayed(hy, sides[k])
        for d in direct(hy, sides[k]):
            spread[k, d].wait_recv()
            block = buf.at[c, yn(-d)]
            for sgn, far in relays:
                if d == 2 * sgn:
                    spread[k, far * sgn] = send(block, block, to_y((far - 2) * sgn))
            share(buf, k, -d)

    def spread_end(buf, k):
        for sgn, far in relayed(hy, sides[k]):
            spread[k, far * sgn].wait_recv()
            share(buf, k, -far * sgn)

    def shared_all(k):
        for key, copy in shared.items():
            if key[0] == k:
                copy.wait_recv()

    spread_first(act_all, 0)
    grad_act = ring_end(1)
    gp_all[c, y] = (grad_act * gelu_slope(preact)).astype(BF16)
    spread_first(gp_all, 1)
    spread_second(gp_all, 1)
    spread_end(gp_all, 1)
    spread_second(act_all, 0)
    shared_all(1)

    grads = gp_all[...].reshape(total, hid)

    def row_terms(span):
        out = lax.dot_general(
            grads, w_in[span, :], (((1,), (1,)), ((), ())), preferred_element_type=F32
        ).reshape(nz, nx, rows, span.size)
        g_full[:, :, :, span] = out
        g_send[:, :, :, span] = out.astype(BF16)

    tx, tl, tr, tf = {}, {}, {}, {}

    def right_first():
        for sgn, d in relayed(hz, 1):
            o = d * sgn
            tr[o] = (send(g_send.at[slot[o], :, :, right], rz_in.at[len(tr)], to_z((d - 2) * sgn)), len(tr))
        for o in direct(hz, 1):
            if abs(o) == 1:
                tr[o] = (send(g_send.at[slot[o], :, :, right], rz_in.at[len(tr)], to_z(o)), len(tr))

    def right_got(o):
        copy, i = tr[o]
        copy.wait_recv()
        return rz_in[i].astype(F32)

    def right_second():
        for i, o in enumerate(d for d in direct(hz, 1) if abs(d) == 2):
            value = g_full[slot[o], :, :, right]
            for sgn, d in relayed(hz, 1):
                if sgn * o > 0:
                    value = value + right_got(d * sgn)
            rz_out[i] = value.astype(BF16)
            tr[o] = (send(rz_out.at[i], rz_in.at[len(tr)], to_z(o)), len(tr))

    def right_end():
        value = g_full[0, :, :, right]
        for o in reversed(direct(hz, 1)):
            value = value + right_got(o)
        rx_sum[...] = value
        for j in range(1, nx):
            tf[j] = send(rx_sum.at[j], rx_in.at[j - 1], to_x(j))

    def left_first():
        value = g_full[:, 0, :, left]
        for j in range(1, nx):
            tx[j].wait_recv()
            value = value + lx_in[j - 1].astype(F32)
        lz_sum[...] = value
        for sgn, d in relayed(hz, -1):
            o = d * sgn
            tl[o] = (send(lz_sum.at[slot[o]], lz_in.at[len(tl)], to_z((d - 2) * sgn)), len(tl))
        for o in direct(hz, -1):
            if abs(o) == 1:
                tl[o] = (send(lz_sum.at[slot[o]], lz_in.at[len(tl)], to_z(o)), len(tl))

    def left_got(o):
        copy, i = tl[o]
        copy.wait_recv()
        return lz_in[i]

    def left_second():
        for i, o in enumerate(d for d in direct(hz, -1) if abs(d) == 2):
            value = lz_sum[slot[o]]
            for sgn, d in relayed(hz, -1):
                if sgn * o > 0:
                    value = value + left_got(d * sgn)
            lz_out[i] = value
            tl[o] = (send(lz_out.at[i], lz_in.at[len(tl)], to_z(o)), len(tl))

    def left_end():
        value = lz_sum[0]
        for o in reversed(direct(hz, -1)):
            value = value + left_got(o)
        grad_tokens[:, left] = value.astype(BF16)

    def weight_in_grad(i, n):
        step = feat // n
        tok = tok_all[:, :, :, i * step : (i + 1) * step].reshape(total, step)
        gwi[i * step : (i + 1) * step, :] = lax.dot_general(
            tok, grads, (((0,), (0,)), ((), ())), preferred_element_type=F32
        ).astype(BF16)

    def weight_out_grad(i, n):
        step = hid // n
        act = act_all[:, :, :, i * step : (i + 1) * step].reshape(total, step)
        gwo[i * step : (i + 1) * step, :] = lax.dot_general(
            act, og_all[...].reshape(total, feat), (((0,), (0,)), ((), ())), preferred_element_type=F32
        ).astype(BF16)

    row_terms(right)
    right_first()
    row_terms(left)
    for j in range(1, nx):
        tx[j] = send(g_send.at[:, j, :, left], lx_in.at[j - 1], to_x(j))
    spread_end(act_all, 0)
    weight_in_grad(0, 3)
    right_second()
    left_first()
    weight_in_grad(1, 3)
    grad_bias[...] = jnp.sum(grads.astype(F32), axis=0, keepdims=True)
    left_second()
    right_end()
    weight_in_grad(2, 3)
    store_in = local(gwi, grad_weight_in, 2)
    shared_all(0)
    for i in range(3):
        weight_out_grad(i, 3)
    store_out = local(gwo, grad_weight_out, 3)
    left_end()
    value = rx_sum[0]
    for j in range(1, nx):
        tf[j].wait_recv()
        value = value + rx_in[j - 1]
    grad_tokens[:, right] = value.astype(BF16)
    store_in.wait()
    store_out.wait()
    for copy in pending:
        copy.wait_send()


def body(nz, ny, tokens, weight_in, bias_in, weight_out, out_grad):
    rows, feat = tokens.shape
    hid = weight_in.shape[1]
    cut = feat // 3 * 2
    rest = feat - cut
    nx = X
    total = nz * nx * rows
    piece = total // (2 * ny)
    vmem, anywhere = pl.BlockSpec(memory_space=pltpu.VMEM), pl.BlockSpec(memory_space=pl.ANY)
    out = pl.pallas_call(
        functools.partial(kernel, nz, ny),
        out_shape=(
            jax.ShapeDtypeStruct((rows, feat), BF16),
            jax.ShapeDtypeStruct((feat, hid), BF16),
            jax.ShapeDtypeStruct((hid, feat), BF16),
            jax.ShapeDtypeStruct((1, hid), F32),
        ),
        in_specs=[anywhere, anywhere, vmem, anywhere, anywhere],
        out_specs=(vmem, anywhere, anywhere, vmem),
        scratch_shapes=[
            pltpu.VMEM((nz, nx, rows, feat), BF16),
            pltpu.VMEM((nz, nx, rows, feat), BF16),
            pltpu.VMEM((feat, hid), BF16),
            pltpu.VMEM((hid, feat), BF16),
            pltpu.VMEM((2, ny, piece, hid), F32),
            pltpu.VMEM((2, ny, piece, hid), F32),
            pltpu.VMEM((2, ny, piece, hid), F32),
            pltpu.VMEM((2, ny - 1, piece, hid), BF16),
            pltpu.VMEM((2, ny - 1, piece, hid), BF16),
            pltpu.VMEM((2, ny, piece, hid), BF16),
            pltpu.VMEM((2, ny, piece, hid), BF16),
            pltpu.VMEM((nz, nx, rows, feat), F32),
            pltpu.VMEM((nz, nx, rows, feat), BF16),
            pltpu.VMEM((nx - 1, nz, rows, cut), BF16),
            pltpu.VMEM((nz, rows, cut), F32),
            pltpu.VMEM((2, rows, cut), F32),
            pltpu.VMEM((nz - 1, rows, cut), F32),
            pltpu.VMEM((2, nx, rows, rest), BF16),
            pltpu.VMEM((nz - 1, nx, rows, rest), BF16),
            pltpu.VMEM((nx, rows, rest), F32),
            pltpu.VMEM((nx - 1, rows, rest), F32),
            pltpu.VMEM((feat, hid), BF16),
            pltpu.VMEM((hid, feat), BF16),
            pltpu.SemaphoreType.DMA((N_SEMS,)),
            pltpu.SemaphoreType.DMA((N_SEMS,)),
            pltpu.SemaphoreType.DMA((4,)),
        ],
        compiler_params=pltpu.CompilerParams(
            collective_id=0, has_side_effects=True, vmem_limit_bytes=56 * 1024 * 1024
        ),
    )(tokens, weight_in, bias_in, weight_out, out_grad)
    return pl.pallas_call(
        copy_out,
        out_shape=(
            jax.ShapeDtypeStruct((rows, feat), BF16),
            jax.ShapeDtypeStruct((feat, hid), BF16),
            jax.ShapeDtypeStruct((hid, feat), BF16),
            jax.ShapeDtypeStruct((hid,), F32),
        ),
        in_specs=[vmem, anywhere, anywhere, vmem],
        out_specs=(vmem, anywhere, anywhere, vmem),
        scratch_shapes=[pltpu.SemaphoreType.DMA((2,))],
        compiler_params=pltpu.CompilerParams(vmem_limit_bytes=56 * 1024 * 1024),
    )(*out)


def solution(mesh):
    nz, ny = mesh.shape["row"] // X, mesh.shape["col"] // 2
    in_specs = (P("row", "col"), P("col", "row"), P("row"), P("row", "col"), P("row", "col"))
    out_specs = (P("row", "col"), P("col", "row"), P("row", "col"), P("row"))
    return jax.shard_map(
        functools.partial(body, nz, ny),
        mesh=mesh,
        in_specs=in_specs,
        out_specs=out_specs,
        check_vma=False,
    )
```

time: 438 us -> 154 us (0.35); the launches traced: 433 us -> 153 us
  waiting for transfers between devices: 281 us -> 0 us
  Pallas kernels: 0 us -> 153 us
  blocking collectives: 120 us -> 0 us
  between operations: 13.8 us -> 0.64 us
  matrix products: 10.9 us -> 0 us
    reduce_scatter x3 -> x0, waiting for transfers between devices: 281 us -> none  [the longest x1 192 us: body(): lax.psum_scatter(input_terms, 'row', scatter_dimension=0, tiled=True)]
    pallas_call x0 -> x2, Pallas kernels: none -> 153 us  [the longest x1 78.9 us: body(): pl.pallas_call(functools.partial(kernel, nz, ny), out_shape=(jax.ShapeDty...]
    all_gather x4 -> x0, blocking collectives: 120 us -> none  [the longest x1 44.7 us: body(): lax.all_gather(out_grad, 'row', axis=0, tiled=True)]
    dot_general x5 -> x0, matrix products: 10.9 us -> none  [the longest x1 3.24 us: body(): lax.dot_general(upstream, weight_out, (((1,), (1,)), ((), ())), preferred...]
  transfers between devices with their start and end apart: 3 -> 0, of which waited for: 3 -> 0; matrix products, arithmetic and copies ran while one was open for 2% -> 0% of each run, Pallas kernels for 0% -> 0%
where the time goes in v1:
time: 154 us; the launch traced here: 153 us
  Pallas kernels  153 us (99%)
    pallas_call x1, Pallas kernels, body(): pl.pallas_call(functools.partial(kernel, nz, ny), out_shape=(jax.ShapeDty...  78.9 us
    pallas_call x1, Pallas kernels, body(): pl.pallas_call(copy_out, out_shape=(jax.ShapeDtypeStruct((rows, feat), BF...  73.9 us

profile of v1, /device:TPU:1, one launch (start us, length us, event | category | flops | bytes accessed | tf_op | source)
XLA Modules:
  0.0 153.5 jit_solution(12771569932031062435)
XLA Ops:
  0.6 78.9 %shard_map.84 = (bf16[16,768]{1,0:T(8,128)(2,1)}, bf16[768,768]{1,0:T(8,128)(2,1)}, bf16[768,768]{1,0:T(8,128)(2,1)}, f32[1,768]{1,0:T(1,128)}) custom-call(bf16[16,768]{1,0:T(8,128)(2,1)} %tokens.1, bf16[768,768]{1,0:T(8,128)(2,1)} %weight_in.1, f32[768]{0:T(1024)} %bias_in.1, bf16[768,768]{1,0:T(8,128)(2,1)} %weight_out.1, bf16[16,768]{1,0:T(8,128)(2,1)} %out_grad.1), custom_call_target="tpu_custom_call" | custom-call | tf_op jit(solution)/shard_map/pallas_call | solution.py:463
  79.6 73.9 %shard_map.85 = (bf16[16,768]{1,0:T(8,128)(2,1)}, bf16[768,768]{1,0:T(8,128)(2,1)}, bf16[768,768]{1,0:T(8,128)(2,1)}, f32[768]{0:T(1024)}) custom-call(bf16[16,768]{1,0:T(8,128)(2,1)} %get-tuple-element.8.a, bf16[768,768]{1,0:T(8,128)(2,1)} %get-tuple-element.9.b, bf16[768,768]{1,0:T(8,128)(2,1)} %get-tuple-element.10.c, f32[1,768]{1,0:T(1,128)} %get-tuple-element.11.d), custom_call_target="tpu_custom_call" | custom-call | tf_op jit(solution)/shard_map/pallas_call | solution.py:505

commit v2 on v1

--- a/solution.py
+++ b/solution.py
@@ -32,17 +32,30 @@
     return out + [n // 2]
 
 
-def copy_out(a, b, c, d, a_out, b_out, c_out, d_out, sems):
-    copies = [
-        pltpu.make_async_copy(src, dst, sems.at[i])
-        for i, (src, dst) in enumerate(((b, b_out), (c, c_out)))
+def copy_out(a, b, c, d, a_out, b_out, c_out, d_out, b_vmem, c_vmem, sems):
+    n = 3
+    step = b.shape[0] // n
+    jobs = [(b, b_vmem, b_out), (c, c_vmem, c_out)]
+    spans = [pl.ds(i * step, step) for i in range(n)]
+    loads = [
+        pltpu.make_async_copy(src.at[span], held.at[span], sems.at[0, i, k])
+        for i, span in enumerate(spans)
+        for k, (src, held, _) in enumerate(jobs)
     ]
-    for copy in copies:
-        copy.start()
+    stores = [
+        pltpu.make_async_copy(held.at[span], dst.at[span], sems.at[1, i, k])
+        for i, span in enumerate(spans)
+        for k, (_, held, dst) in enumerate(jobs)
+    ]
+    for load in loads:
+        load.start()
     a_out[...] = a[...]
     d_out[...] = jnp.sum(d[...], axis=0)
-    for copy in copies:
-        copy.wait()
+    for load, store in zip(loads, stores):
+        load.wait()
+        store.start()
+    for store in stores:
+        store.wait()
 
 
 def kernel(
@@ -163,13 +176,13 @@
     sides = (1, -1)
     rx, lz, lx, rz = ({} for _ in range(4))
 
-    for a, (src, buf) in enumerate(sources):
-        for j in range(1, nx):
-            rx[a, j] = send(src.at[:, right], buf.at[0, nx - j, :, right], to_x(j))
-        for d in direct(hz, sides[a]):
-            lz[a, d] = send(src.at[:, left], buf.at[slot[-d], 0, :, left], to_z(d))
     own_tok.wait()
     own_og.wait()
+    for a, (_, buf) in enumerate(sources):
+        for j in range(1, nx):
+            rx[a, j] = send(buf.at[0, 0, :, right], buf.at[0, nx - j, :, right], to_x(j))
+        for d in direct(hz, sides[a]):
+            lz[a, d] = send(buf.at[0, 0, :, left], buf.at[slot[-d], 0, :, left], to_z(d))
     for a, (_, buf) in enumerate(sources):
         for j in range(1, nx):
             rx[a, j].wait_recv()
@@ -224,25 +237,31 @@
             )
         return out.reshape(ny, piece, hid)
 
-    def order(a):
-        out = [d * sgn for sgn, d in relayed(hy, sides[a])]
-        one = [d for d in direct(hy, sides[a]) if abs(d) == 1]
-        two = [d for d in direct(hy, sides[a]) if abs(d) == 2]
-        return out + one + two + [0]
-
-    pair, ring = {}, {}
+    pair, ring, waited, group = {}, {}, {}, {}
 
     def to_partner(a):
-        pair_out[a] = product(a, 1 - c)
-        for o in order(a):
-            pair[a, o] = send(pair_out.at[a, yn(o)], pair_in.at[a, yn(o)], partner)
+        out = product(a, 1 - c)
+        for i in range(ny):
+            pair_out[a, lax.rem(i + ny - y, ny)] = out[i]
+        lo, hi = (hy - 1, hy + 2) if ny > 4 else (0, ny)
+        for first, last in ((lo, hi), (0, lo), (hi, ny)):
+            if first < last:
+                span = pl.ds(first, last - first)
+                copy = send(pair_out.at[a, span], pair_in.at[a, span], partner)
+                for i in range(first, last):
+                    pair[a, i] = copy
+                    waited[a, first] = False
+                    group[a, i] = first
 
     def keep(a):
         part[a] = product(a, c)
 
     def chip_sum(a, o):
-        pair[a, o].wait_recv()
-        return part[a, yn(o)] + pair_in[a, yn(o)]
+        i = o % ny
+        if not waited[a, group[a, i]]:
+            pair[a, i].wait_recv()
+            waited[a, group[a, i]] = True
+        return part[a, yn(o)] + pair_in[a, i]
 
     def ring_send(a, k, value, d):
         i = len([key for key in ring if key[0] == a])
@@ -294,6 +313,8 @@
     spread, shared = {}, {}
 
     def share(buf, k, o):
+        if k == 0:
+            return
         block = buf.at[c, yn(o)]
         shared[k, o] = send(block, block, partner)
 
@@ -317,6 +338,8 @@
         for sgn, far in relayed(hy, sides[k]):
             spread[k, far * sgn].wait_recv()
             share(buf, k, -far * sgn)
+        if k == 0:
+            shared[0, 0] = send(buf.at[c], buf.at[c], partner)
 
     def shared_all(k):
         for key, copy in shared.items():
@@ -512,7 +535,11 @@
         ),
         in_specs=[vmem, anywhere, anywhere, vmem],
         out_specs=(vmem, anywhere, anywhere, vmem),
-        scratch_shapes=[pltpu.SemaphoreType.DMA((2,))],
+        scratch_shapes=[
+            pltpu.VMEM((feat, hid), BF16),
+            pltpu.VMEM((hid, feat), BF16),
+            pltpu.SemaphoreType.DMA((2, 3, 2)),
+        ],
         compiler_params=pltpu.CompilerParams(vmem_limit_bytes=56 * 1024 * 1024),
     )(*out)
 

time: 154 us -> 83.8 us (0.54)
  Pallas kernels: 153 us -> 82.6 us
    pallas_call x1, Pallas kernels: 73.9 us -> 3.84 us  [body(): pl.pallas_call(copy_out, out_shape=(jax.ShapeDtypeStruct((rows, feat), BF...]
where the time goes in v2:
time: 83.8 us; the launch traced here: 83.3 us
  Pallas kernels  82.6 us (99%)
    pallas_call x1, Pallas kernels, body(): pl.pallas_call(functools.partial(kernel, nz, ny), out_shape=(jax.ShapeDty...  78.8 us
    pallas_call x1, Pallas kernels, body(): pl.pallas_call(copy_out, out_shape=(jax.ShapeDtypeStruct((rows, feat), BF...  3.84 us

profile of v2, /device:TPU:1, one launch (start us, length us, event | category | flops | bytes accessed | tf_op | source)
XLA Modules:
  0.0 83.3 jit_solution(4710357411099968668)
XLA Ops:
  0.6 78.8 %shard_map.84 = (bf16[16,768]{1,0:T(8,128)(2,1)}, bf16[768,768]{1,0:T(8,128)(2,1)}, bf16[768,768]{1,0:T(8,128)(2,1)}, f32[1,768]{1,0:T(1,128)}) custom-call(bf16[16,768]{1,0:T(8,128)(2,1)} %tokens.1, bf16[768,768]{1,0:T(8,128)(2,1)} %weight_in.1, f32[768]{0:T(1024)} %bias_in.1, bf16[768,768]{1,0:T(8,128)(2,1)} %weight_out.1, bf16[16,768]{1,0:T(8,128)(2,1)} %out_grad.1), custom_call_target="tpu_custom_call" | custom-call | tf_op jit(solution)/shard_map/pallas_call | solution.py:486
  79.4 3.8 %shard_map.85 = (bf16[16,768]{1,0:T(8,128)(2,1)}, bf16[768,768]{1,0:T(8,128)(2,1)}, bf16[768,768]{1,0:T(8,128)(2,1)}, f32[768]{0:T(1024)}) custom-call(bf16[16,768]{1,0:T(8,128)(2,1)} %get-tuple-element.8.a, bf16[768,768]{1,0:T(8,128)(2,1)} %get-tuple-element.9.b, bf16[768,768]{1,0:T(8,128)(2,1)} %get-tuple-element.10.c, f32[1,768]{1,0:T(1,128)} %get-tuple-element.11.d), custom_call_target="tpu_custom_call" | custom-call | tf_op jit(solution)/shard_map/pallas_call | solution.py:528

commit v3 on v2

v3 whole, which is shorter than its diff:
```python
import functools

import jax
import jax.numpy as jnp
from jax import lax
from jax.experimental import pallas as pl
from jax.experimental.pallas import tpu as pltpu
from jax.sharding import PartitionSpec as P

SQRT_HALF = 0.7071067811865476
INV_ROOT_TWO_PI = 0.3989422804014327
X = 4
N_SEMS = 192
CHUNKS = 2
BF16, F32 = jnp.bfloat16, jnp.float32
MESH = pl.DeviceIdType.MESH


def gelu_value(preact):
    return preact * 0.5 * (1.0 + lax.erf(preact * SQRT_HALF))


def gelu_slope(preact):
    return 0.5 * (1.0 + lax.erf(preact * SQRT_HALF)) + preact * INV_ROOT_TWO_PI * jnp.exp(
        -0.5 * preact * preact
    )


def around(n):
    out = [0]
    for d in range(1, n // 2):
        out += [d, -d]
    return out + [n // 2]


def copy_out(a, b, c, d, a_out, b_out, c_out, d_out, b_vmem, c_vmem, sems):
    n = 3
    step = b.shape[0] // n
    jobs = [(b, b_vmem, b_out), (c, c_vmem, c_out)]
    spans = [pl.ds(i * step, step) for i in range(n)]
    loads = [
        pltpu.make_async_copy(src.at[span], held.at[span], sems.at[0, i, k])
        for i, span in enumerate(spans)
        for k, (src, held, _) in enumerate(jobs)
    ]
    stores = [
        pltpu.make_async_copy(held.at[span], dst.at[span], sems.at[1, i, k])
        for i, span in enumerate(spans)
        for k, (_, held, dst) in enumerate(jobs)
    ]
    for load in loads:
        load.start()
    a_out[...] = a[...]
    d_out[...] = jnp.sum(d[...], axis=0)
    for load, store in zip(loads, stores):
        load.wait()
        store.start()
    for store in stores:
        store.wait()


def kernel(
    nz,
    ny,
    chunks,
    tokens,
    weight_in,
    bias_in,
    weight_out,
    out_grad,
    grad_tokens,
    grad_weight_in,
    grad_weight_out,
    grad_bias,
    tok_half,
    og_half,
    tok_other,
    og_other,
    stage,
    own_right,
    w_in,
    w_out,
    part,
    ring_out,
    ring_in,
    act_all,
    gp_all,
    g_full,
    g_send,
    lx_in,
    lz_sum,
    lz_out,
    lz_in,
    rz_out,
    rz_in,
    rx_sum,
    rx_in,
    gwi,
    gwo,
    send_sems,
    recv_sems,
    slot_sems,
    local_sems,
):
    nx = X
    nxs = nx // 2
    rows, feat = tokens.shape
    hid = w_in.shape[-1]
    cut = stage.shape[-1]
    rest = feat - cut
    pr = nz * rows // ny
    hz, hy = nz // 2, ny // 2
    per = nxs // chunks
    spans = [pl.ds(k * per, per) for k in range(chunks)]
    row, col = lax.axis_index("row"), lax.axis_index("col")
    z, x = lax.div(row, nx), lax.rem(row, nx)
    y, c = lax.div(col, 2), lax.rem(col, 2)
    first_core, second_core = c == 0, c == 1

    def yn(d):
        return lax.rem(y + (ny + d), ny)

    def to_z(d):
        return (lax.rem(z + (nz + d), nz) * nx + x, col)

    def to_x(j, core):
        return (z * nx + lax.rem(x + j, nx), y * 2 + core)

    def to_y(d):
        return (row, yn(d) * 2 + c)

    partner = (row, y * 2 + (1 - c))
    pending = []
    slot_ids = {}

    def slot_id(key, count):
        if key not in slot_ids:
            slot_ids[key] = sum(n for _, n in slot_ids.values()), count
        return slot_ids[key][0]

    def send(src, dst, device, recv_sem=None, only=None):
        i = len(pending)
        copy = pltpu.make_async_remote_copy(
            src_ref=src,
            dst_ref=dst,
            send_sem=send_sems.at[i],
            recv_sem=recv_sems.at[i] if recv_sem is None else recv_sem,
            device_id=device,
            device_id_type=MESH,
        )
        if only is None:
            copy.start()
        else:
            pl.when(only)(copy.start)
        pending.append((copy, only))
        return copy

    def landed(dst, sem, only=None):
        copy = pltpu.make_async_remote_copy(
            src_ref=dst,
            dst_ref=dst,
            send_sem=send_sems.at[0],
            recv_sem=sem,
            device_id=partner,
            device_id_type=MESH,
        )
        if only is None:
            copy.wait_recv()
        else:
            pl.when(only)(copy.wait_recv)

    def local(src, dst, i):
        copy = pltpu.make_async_copy(src, dst, local_sems.at[i])
        copy.start()
        return copy

    left, right = pl.ds(0, cut), pl.ds(cut, rest)
    slot = {d: i for i, d in enumerate(around(nz))}
    slot[-hz] = slot[hz]
    near = 2 * min(hz, 3) - 1
    batches = [pl.ds(0, near)] + [pl.ds(near, nz - near)] * (near < nz)

    def direct(h, side):
        out = []
        for d in (2, 1):
            if d < h:
                out += [d, -d]
            elif d == h:
                out.append(d * side)
        return out

    def relayed(h, side):
        return [(sgn, d) for sgn in (1, -1) for d in (3, 4) if d < h or (d == h and sgn == side)]

    sources = ((tokens, tok_half), (out_grad, og_half))
    sides = (1, -1)
    own = []
    for a, (src, _) in enumerate(sources):
        own.append(local(src.at[:, left], stage.at[a, 0], 2 * a))
        own.append(local(src.at[:, right], own_right.at[a], 2 * a + 1))
    load_in = local(weight_in, w_in.at[c], 4)
    load_out = local(weight_out, w_out.at[c], 5)

    barrier = pltpu.get_barrier_semaphore()
    friends = [to_x(j, core) for j in range(1, nx) for core in (0, 1)] + [partner]
    for d in (1, -1, 2, -2):
        friends += [to_z(d)] * (abs(d) <= hz) + [to_y(d)] * (abs(d) <= hy)
    for device in friends:
        pl.semaphore_signal(barrier, inc=1, device_id=device, device_id_type=MESH)
    pl.semaphore_wait(barrier, len(friends))
    for copy in own:
        copy.wait()

    lz, rz = {}, {}
    hops = sorted(range(1, nx), key=lambda j: (nx - j) % nxs)

    def x_sem(a, kind, xs, block):
        return slot_sems.at[slot_id((a, kind, xs), 2) + block]

    def over_x(a, kind, src, dst):
        for j in [0] + hops:
            core, xs = divmod((nx - j) % nx, nxs)
            if j == 0:
                send(src, dst(0, 1), partner, x_sem(a, kind, 0, 1), second_core)
            else:
                send(src, dst(xs, c), to_x(j, core), x_sem(a, kind, xs, c))

    def from_x(a, kind, xs, dst):
        for block in (0, 1):
            only = second_core if (xs, block) == (0, 0) else None
            landed(dst(xs, block), x_sem(a, kind, xs, block), only)

    def right_at(a):
        buf = sources[a][1]
        return lambda xs, block: buf.at[xs, block, 0, :, right]

    def left_at(a, zs):
        buf = sources[a][1]
        return lambda xs, block: buf.at[xs, block, zs, :, left]

    def right_block(a, k, s):
        return sources[a][1].at[spans[k], :, s, :, right]

    for a in (0, 1):
        over_x(a, "r", own_right.at[a], right_at(a))
        for d in direct(hz, sides[a]):
            lz[a, d] = send(stage.at[a, 0], stage.at[a, slot[-d]], to_z(d))

    @pl.when(first_core)
    def _():
        for a, (_, buf) in enumerate(sources):
            buf[0, 0, 0, :, right] = own_right[a]

    load_in.wait()
    send_in = send(w_in.at[c], w_in.at[c], partner)
    load_out.wait()
    send_out = send(w_out.at[c], w_out.at[c], partner)

    for k in range(chunks):
        for a in (0, 1):
            for xs in range(k * per, (k + 1) * per):
                from_x(a, "r", xs, right_at(a))
            for d in direct(hz, sides[a]):
                rz[a, k, d] = send(right_block(a, k, 0), right_block(a, k, slot[-d]), to_z(d))
    for a in (0, 1):
        for sgn, d in relayed(hz, sides[a]):
            if d == 3:
                lz[a, 2 * sgn].wait_recv()
            lz[a, d * sgn] = send(
                stage.at[a, slot[-2 * sgn]], stage.at[a, slot[-d * sgn]], to_z((d - 2) * sgn)
            )
        for d in direct(hz, sides[a]):
            if not (hz > 2 and abs(d) == 2):
                lz[a, d].wait_recv()
        over_x(a, 0, stage.at[a, batches[0]], left_at(a, batches[0]))
    for k in range(chunks):
        for a in (0, 1):
            for sgn, d in relayed(hz, sides[a]):
                if d == 3:
                    rz[a, k, 2 * sgn].wait_recv()
                rz[a, k, d * sgn] = send(
                    right_block(a, k, slot[-2 * sgn]),
                    right_block(a, k, slot[-d * sgn]),
                    to_z((d - 2) * sgn),
                )
    for a in (0, 1):
        for sgn, d in relayed(hz, sides[a]):
            lz[a, d * sgn].wait_recv()
        if near < nz:
            over_x(a, 1, stage.at[a, batches[1]], left_at(a, batches[1]))

    @pl.when(first_core)
    def _():
        for a, (_, buf) in enumerate(sources):
            buf[0, 0, :, :, left] = stage[a]

    def gathered(a, k):
        for d in direct(hz, sides[a]):
            if not (hz > 2 and abs(d) == 2):
                rz[a, k, d].wait_recv()
        for sgn, d in relayed(hz, sides[a]):
            rz[a, k, d * sgn].wait_recv()
        for xs in range(k * per, (k + 1) * per):
            for i, zs in enumerate(batches):
                from_x(a, i, xs, left_at(a, zs))

    def product(a, k):
        total = 0
        for block in (0, 1):
            lhs = sources[a][1][spans[k], block].reshape(per * nz * rows, feat)
            if a == 0:
                out = jnp.dot(lhs, w_in[block], preferred_element_type=F32)
            else:
                out = lax.dot_general(
                    lhs, w_out[block], (((1,), (1,)), ((), ())), preferred_element_type=F32
                )
            total = out if block == 0 else total + out
        part[a, spans[k]] = total.reshape(per, ny, pr, hid)

    ring = {}

    def ring_send(a, k, o, value, d):
        i = len([key for key in ring if key[:2] == (a, k)])
        ring_out[a, k, i] = value.astype(BF16)
        ring[a, k, o] = (send(ring_out.at[a, k, i], ring_in.at[a, k, i], to_y(d)), i)

    def ring_got(a, k, o):
        copy, i = ring[a, k, o]
        copy.wait_recv()
        return ring_in[a, k, i].astype(F32)

    def ring_first(a, k):
        for sgn, d in relayed(hy, sides[a]):
            ring_send(a, k, d * sgn, part[a, spans[k], yn(d * sgn)], (d - 2) * sgn)
        for d in direct(hy, sides[a]):
            if abs(d) == 1:
                ring_send(a, k, d, part[a, spans[k], yn(d)], d)

    def ring_second(a, k):
        for d in direct(hy, sides[a]):
            if abs(d) == 2:
                value = part[a, spans[k], yn(d)]
                for sgn, far in relayed(hy, sides[a]):
                    if sgn * d > 0:
                        value = value + ring_got(a, k, far * sgn)
                ring_send(a, k, d, value, d)

    def ring_end(a, k):
        value = part[a, spans[k], y]
        for d in reversed(direct(hy, sides[a])):
            value = value + ring_got(a, k, d)
        return value

    for k in range(chunks):
        for a in (0, 1):
            gathered(a, k)
            if k == 0:
                (send_in, send_out)[a].wait_recv()
            product(a, k)
            ring_first(a, k)
    shared = []
    for a, other in enumerate((tok_other, og_other)):
        shared.append(send(sources[a][1].at[:, 1 - c], other, partner))
    for k in range(chunks):
        ring_second(0, k)
        ring_second(1, k)

    spread = {}

    def spread_first(buf, a, k):
        for d in direct(hy, sides[a]):
            block = buf.at[c, spans[k], y]
            spread[a, k, d] = send(block, block, to_y(d))

    def spread_second(buf, a, k):
        for d in direct(hy, sides[a]):
            spread[a, k, d].wait_recv()
            block = buf.at[c, spans[k], yn(-d)]
            for sgn, far in relayed(hy, sides[a]):
                if d == 2 * sgn:
                    spread[a, k, far * sgn] = send(block, block, to_y((far - 2) * sgn))

    def spread_end(a, k):
        for sgn, far in relayed(hy, sides[a]):
            spread[a, k, far * sgn].wait_recv()

    for k in range(chunks):
        preact = ring_end(0, k) + bias_in[...][None, None, :]
        act_all[c, spans[k], y] = gelu_value(preact).astype(BF16)
        slope = gelu_slope(preact)
        gp_all[c, spans[k], y] = (ring_end(1, k) * slope).astype(BF16)
        spread_first(gp_all, 1, k)
    for k in range(chunks):
        spread_second(gp_all, 1, k)
    for k in range(chunks):
        spread_first(act_all, 0, k)

    def row_terms(k, span):
        grads = gp_all[c, spans[k]].reshape(per * nz * rows, hid)
        for block in (0, 1):
            out = lax.dot_general(
                grads, w_in[block, span, :], (((1,), (1,)), ((), ())), preferred_element_type=F32
            ).reshape(per, nz, rows, span.size)
            g_full[spans[k], block, :, :, span] = out
            g_send[spans[k], block, :, :, span] = out.astype(BF16)

    tl, tr = {}, {}

    def home(kind, k, src, dst):
        for xs in range(k * per, (k + 1) * per):
            s = c * nxs + xs
            for block in (0, 1):
                sem = slot_sems.at[slot_id(kind, nx) + s]
                only = second_core if (xs, block) == (0, 0) else None
                send(src(xs, block), dst.at[s], to_x(s, block), sem, only)

    def at_home(kind, dst):
        for s in range(nx):
            sem = slot_sems.at[slot_id(kind, nx) + s]
            landed(dst.at[s], sem, second_core if s == 0 else None)

    def right_put(k, o, src, d):
        i = len([key for key in tr if key[0] == k])
        tr[k, o] = (send(src, rz_in.at[k, i], to_z(d)), i)

    def right_got(k, o):
        copy, i = tr[k, o]
        copy.wait_recv()
        return rz_in[k, i].astype(F32)

    def right_first(k):
        for sgn, d in relayed(hz, 1):
            o = d * sgn
            right_put(k, o, g_send.at[spans[k], :, slot[o], :, right], (d - 2) * sgn)
        for o in direct(hz, 1):
            if abs(o) == 1:
                right_put(k, o, g_send.at[spans[k], :, slot[o], :, right], o)

    def right_second(k):
        for i, o in enumerate(d for d in direct(hz, 1) if abs(d) == 2):
            value = g_full[spans[k], :, slot[o], :, right]
            for sgn, d in relayed(hz, 1):
                if sgn * o > 0:
                    value = value + right_got(k, d * sgn)
            rz_out[k, i] = value.astype(BF16)
            right_put(k, o, rz_out.at[k, i], o)

    def right_end(k):
        value = g_full[spans[k], :, 0, :, right]
        for o in reversed(direct(hz, 1)):
            value = value + right_got(k, o)
        rx_sum[spans[k]] = value
        home("right", k, lambda xs, block: rx_sum.at[xs, block], rx_in)

    def left_put(o, src, d):
        tl[o] = (send(src, lz_in.at[len(tl)], to_z(d)), len(tl))

    def left_got(o):
        copy, i = tl[o]
        copy.wait_recv()
        return lz_in[i]

    def left_first():
        at_home("left", lx_in)

        @pl.when(first_core)
        def _():
            lx_in[0] = g_send[0, 0, :, :, left]

        value = lx_in[0].astype(F32)
        for s in range(1, nx):
            value = value + lx_in[s].astype(F32)
        lz_sum[...] = value
        for sgn, d in relayed(hz, -1):
            left_put(d * sgn, lz_sum.at[slot[d * sgn]], (d - 2) * sgn)
        for o in direct(hz, -1):
            if abs(o) == 1:
                left_put(o, lz_sum.at[slot[o]], o)

    def left_second():
        for i, o in enumerate(d for d in direct(hz, -1) if abs(d) == 2):
            value = lz_sum[slot[o]]
            for sgn, d in relayed(hz, -1):
                if sgn * o > 0:
                    value = value + left_got(d * sgn)
            lz_out[i] = value
            left_put(o, lz_out.at[i], o)

    def left_end():
        value = lz_sum[0]
        for o in reversed(direct(hz, -1)):
            value = value + left_got(o)
        grad_tokens[:, left] = value.astype(BF16)

    half = nxs * nz * rows

    def weight_in_grad(i, n):
        step = feat // n
        span = pl.ds(i * step, step)
        out = lax.dot_general(
            tok_half[:, c, :, :, span].reshape(half, step),
            gp_all[c].reshape(half, hid),
            (((0,), (0,)), ((), ())),
            preferred_element_type=F32,
        ) + lax.dot_general(
            tok_other[:, :, :, span].reshape(half, step),
            gp_all[1 - c].reshape(half, hid),
            (((0,), (0,)), ((), ())),
            preferred_element_type=F32,
        )
        gwi[span, :] = out.astype(BF16)

    def weight_out_grad(i, n):
        step = hid // n
        span = pl.ds(i * step, step)
        out = lax.dot_general(
            act_all[c, :, :, :, span].reshape(half, step),
            og_half[:, c].reshape(half, feat),
            (((0,), (0,)), ((), ())),
            preferred_element_type=F32,
        ) + lax.dot_general(
            act_all[1 - c, :, :, :, span].reshape(half, step),
            og_other[...].reshape(half, feat),
            (((0,), (0,)), ((), ())),
            preferred_element_type=F32,
        )
        gwo[span, :] = out.astype(BF16)

    for k in range(chunks):
        spread_end(1, k)
        row_terms(k, right)
        right_first(k)
        row_terms(k, left)
        home("left", k, lambda xs, block: g_send.at[xs, block, :, :, left], lx_in)
    shared.append(send(gp_all.at[c], gp_all.at[c], partner))
    for k in range(chunks):
        spread_second(act_all, 0, k)
    for k in range(chunks):
        right_second(k)
    left_first()
    for copy in shared:
        copy.wait_recv()
    weight_in_grad(0, 3)
    for k in range(chunks):
        spread_end(0, k)
    share_act = send(act_all.at[c], act_all.at[c], partner)
    for k in range(chunks):
        right_end(k)
    left_second()
    for i in (1, 2):
        weight_in_grad(i, 3)
    store_in = local(gwi, grad_weight_in, 4)
    grad_bias[...] = jnp.sum(gp_all[...].astype(F32).reshape(2 * half, hid), axis=0, keepdims=True)
    share_act.wait_recv()
    for i in range(3):
        weight_out_grad(i, 3)
    store_out = local(gwo, grad_weight_out, 5)
    left_end()
    at_home("right", rx_in)

    @pl.when(first_core)
    def _():
        rx_in[0] = rx_sum[0, 0]

    value = rx_in[0]
    for s in range(1, nx):
        value = value + rx_in[s]
    grad_tokens[:, right] = value.astype(BF16)
    store_in.wait()
    store_out.wait()
    for copy, only in pending:
        if only is None:
            copy.wait_send()
        else:
            pl.when(only)(copy.wait_send)


def body(nz, ny, tokens, weight_in, bias_in, weight_out, out_grad):
    rows, feat = tokens.shape
    hid = weight_in.shape[1]
    cut = feat // 3 * 2
    rest = feat - cut
    nx = X
    nxs = nx // 2
    chunks = min(CHUNKS, nxs)
    per = nxs // chunks
    pr = nz * rows // ny
    vmem, anywhere = pl.BlockSpec(memory_space=pltpu.VMEM), pl.BlockSpec(memory_space=pl.ANY)
    out = pl.pallas_call(
        functools.partial(kernel, nz, ny, chunks),
        out_shape=(
            jax.ShapeDtypeStruct((rows, feat), BF16),
            jax.ShapeDtypeStruct((feat, hid), BF16),
            jax.ShapeDtypeStruct((hid, feat), BF16),
            jax.ShapeDtypeStruct((1, hid), F32),
        ),
        in_specs=[anywhere, anywhere, vmem, anywhere, anywhere],
        out_specs=(vmem, anywhere, anywhere, vmem),
        scratch_shapes=[
            pltpu.VMEM((nxs, 2, nz, rows, feat), BF16),
            pltpu.VMEM((nxs, 2, nz, rows, feat), BF16),
            pltpu.VMEM((nxs, nz, rows, feat), BF16),
            pltpu.VMEM((nxs, nz, rows, feat), BF16),
            pltpu.VMEM((2, nz, rows, cut), BF16),
            pltpu.VMEM((2, rows, rest), BF16),
            pltpu.VMEM((2, feat, hid), BF16),
            pltpu.VMEM((2, hid, feat), BF16),
            pltpu.VMEM((2, nxs, ny, pr, hid), F32),
            pltpu.VMEM((2, chunks, ny - 1, per, pr, hid), BF16),
            pltpu.VMEM((2, chunks, ny - 1, per, pr, hid), BF16),
            pltpu.VMEM((2, nxs, ny, pr, hid), BF16),
            pltpu.VMEM((2, nxs, ny, pr, hid), BF16),
            pltpu.VMEM((nxs, 2, nz, rows, feat), F32),
            pltpu.VMEM((nxs, 2, nz, rows, feat), BF16),
            pltpu.VMEM((nx, nz, rows, cut), BF16),
            pltpu.VMEM((nz, rows, cut), F32),
            pltpu.VMEM((2, rows, cut), F32),
            pltpu.VMEM((nz - 1, rows, cut), F32),
            pltpu.VMEM((chunks, 2, per, 2, rows, rest), BF16),
            pltpu.VMEM((chunks, nz - 1, per, 2, rows, rest), BF16),
            pltpu.VMEM((nxs, 2, rows, rest), F32),
            pltpu.VMEM((nx, rows, rest), F32),
            pltpu.VMEM((feat, hid), BF16),
            pltpu.VMEM((hid, feat), BF16),
            pltpu.SemaphoreType.DMA((N_SEMS,)),
            pltpu.SemaphoreType.DMA((N_SEMS,)),
            pltpu.SemaphoreType.DMA((64,)),
            pltpu.SemaphoreType.DMA((6,)),
        ],
        compiler_params=pltpu.CompilerParams(
            collective_id=0, has_side_effects=True, vmem_limit_bytes=56 * 1024 * 1024
        ),
    )(tokens, weight_in, bias_in, weight_out, out_grad)
    return pl.pallas_call(
        copy_out,
        out_shape=(
            jax.ShapeDtypeStruct((rows, feat), BF16),
            jax.ShapeDtypeStruct((feat, hid), BF16),
            jax.ShapeDtypeStruct((hid, feat), BF16),
            jax.ShapeDtypeStruct((hid,), F32),
        ),
        in_specs=[vmem, anywhere, anywhere, vmem],
        out_specs=(vmem, anywhere, anywhere, vmem),
        scratch_shapes=[
            pltpu.VMEM((feat, hid), BF16),
            pltpu.VMEM((hid, feat), BF16),
            pltpu.SemaphoreType.DMA((2, 3, 2)),
        ],
        compiler_params=pltpu.CompilerParams(vmem_limit_bytes=56 * 1024 * 1024),
    )(*out)


def solution(mesh):
    nz, ny = mesh.shape["row"] // X, mesh.shape["col"] // 2
    in_specs = (P("row", "col"), P("col", "row"), P("row"), P("row", "col"), P("row", "col"))
    out_specs = (P("row", "col"), P("col", "row"), P("row", "col"), P("row"))
    return jax.shard_map(
        functools.partial(body, nz, ny),
        mesh=mesh,
        in_specs=in_specs,
        out_specs=out_specs,
        check_vma=False,
    )
```

time: 83.8 us -> 78.4 us (0.936)
  Pallas kernels: 82.6 us -> 77.5 us
    pallas_call x1, Pallas kernels: 78.8 us -> 73.6 us  [body(): pl.pallas_call(functools.partial(kernel, nz, ny, chunks), out_shape=(jax....]
where the time goes in v3:
time: 78.4 us; the launch traced here: 78.1 us
  Pallas kernels  77.5 us (99%)
    pallas_call x1, Pallas kernels, body(): pl.pallas_call(functools.partial(kernel, nz, ny, chunks), out_shape=(jax....  73.6 us
    pallas_call x1, Pallas kernels, body(): pl.pallas_call(copy_out, out_shape=(jax.ShapeDtypeStruct((rows, feat), BF...  3.84 us

profile of v3, /device:TPU:1, one launch (start us, length us, event | category | flops | bytes accessed | tf_op | source)
XLA Modules:
  0.0 78.1 jit_solution(15862135510396635284)
XLA Ops:
  0.6 73.6 %shard_map.84 = (bf16[16,768]{1,0:T(8,128)(2,1)}, bf16[768,768]{1,0:T(8,128)(2,1)}, bf16[768,768]{1,0:T(8,128)(2,1)}, f32[1,768]{1,0:T(1,128)}) custom-call(bf16[16,768]{1,0:T(8,128)(2,1)} %tokens.1, bf16[768,768]{1,0:T(8,128)(2,1)} %weight_in.1, f32[768]{0:T(1024)} %bias_in.1, bf16[768,768]{1,0:T(8,128)(2,1)} %weight_out.1, bf16[16,768]{1,0:T(8,128)(2,1)} %out_grad.1), custom_call_target="tpu_custom_call" | custom-call | tf_op jit(solution)/shard_map/pallas_call | solution.py:589
  74.3 3.8 %shard_map.85 = (bf16[16,768]{1,0:T(8,128)(2,1)}, bf16[768,768]{1,0:T(8,128)(2,1)}, bf16[768,768]{1,0:T(8,128)(2,1)}, f32[768]{0:T(1024)}) custom-call(bf16[16,768]{1,0:T(8,128)(2,1)} %get-tuple-element.8.a, bf16[768,768]{1,0:T(8,128)(2,1)} %get-tuple-element.9.b, bf16[768,768]{1,0:T(8,128)(2,1)} %get-tuple-element.10.c, f32[1,768]{1,0:T(1,128)} %get-tuple-element.11.d), custom_call_target="tpu_custom_call" | custom-call | tf_op jit(solution)/shard_map/pallas_call | solution.py:634

commit v4 on v3

--- a/solution.py
+++ b/solution.py
@@ -12,6 +12,7 @@
 X = 4
 N_SEMS = 192
 CHUNKS = 2
+LIMIT = 56 * 1024 * 1024
 BF16, F32 = jnp.bfloat16, jnp.float32
 MESH = pl.DeviceIdType.MESH
 
@@ -33,30 +34,12 @@
     return out + [n // 2]
 
 
-def copy_out(a, b, c, d, a_out, b_out, c_out, d_out, b_vmem, c_vmem, sems):
-    n = 3
-    step = b.shape[0] // n
-    jobs = [(b, b_vmem, b_out), (c, c_vmem, c_out)]
-    spans = [pl.ds(i * step, step) for i in range(n)]
-    loads = [
-        pltpu.make_async_copy(src.at[span], held.at[span], sems.at[0, i, k])
-        for i, span in enumerate(spans)
-        for k, (src, held, _) in enumerate(jobs)
-    ]
-    stores = [
-        pltpu.make_async_copy(held.at[span], dst.at[span], sems.at[1, i, k])
-        for i, span in enumerate(spans)
-        for k, (_, held, dst) in enumerate(jobs)
-    ]
-    for load in loads:
-        load.start()
-    a_out[...] = a[...]
-    d_out[...] = jnp.sum(d[...], axis=0)
-    for load, store in zip(loads, stores):
-        load.wait()
-        store.start()
-    for store in stores:
-        store.wait()
+def copy_out(*refs):
+    copies = [pltpu.make_async_copy(refs[i], refs[4 + i], refs[8].at[i]) for i in (1, 2, 0, 3)]
+    for copy in copies:
+        copy.start()
+    for copy in copies:
+        copy.wait()
 
 
 def kernel(
@@ -95,8 +78,6 @@
     rz_in,
     rx_sum,
     rx_in,
-    gwi,
-    gwo,
     send_sems,
     recv_sems,
     slot_sems,
@@ -112,6 +93,7 @@
     hz, hy = nz // 2, ny // 2
     per = nxs // chunks
     spans = [pl.ds(k * per, per) for k in range(chunks)]
+    turns = range(chunks - 1, -1, -1)
     row, col = lax.axis_index("row"), lax.axis_index("col")
     z, x = lax.div(row, nx), lax.rem(row, nx)
     y, c = lax.div(col, 2), lax.rem(col, 2)
@@ -214,18 +196,48 @@
     lz, rz = {}, {}
     hops = sorted(range(1, nx), key=lambda j: (nx - j) % nxs)
 
+    def far_relay(kind):
+        return nx == 4 and kind != "r"
+
+    holders = ((second_core, first_core), (first_core, second_core))
+
+    def relay_x(a, kind, zs):
+        if not far_relay(kind):
+            return
+        buf = sources[a][1]
+        holder = holders[a][0]
+        for block in (0, 1):
+            landed(buf.at[1, block, zs, :, left], x_sem(a, kind, 1, block), holder)
+        send(
+            buf.at[1, :, zs, :, left],
+            buf.at[0, :, zs, :, left],
+            to_x(1 if a == 0 else nx - 1, 1),
+            slot_sems.at[slot_id((a, kind, "far"), 1)],
+            holder,
+        )
+
     def x_sem(a, kind, xs, block):
         return slot_sems.at[slot_id((a, kind, xs), 2) + block]
 
     def over_x(a, kind, src, dst):
         for j in [0] + hops:
             core, xs = divmod((nx - j) % nx, nxs)
+            if far_relay(kind) and j == nx // 2:
+                continue
             if j == 0:
                 send(src, dst(0, 1), partner, x_sem(a, kind, 0, 1), second_core)
             else:
                 send(src, dst(xs, c), to_x(j, core), x_sem(a, kind, xs, c))
 
     def from_x(a, kind, xs, dst):
+        if far_relay(kind):
+            if xs == 0:
+                landed(dst(0, 1), x_sem(a, kind, 0, 1), first_core)
+                landed(dst(0, slice(None)), slot_sems.at[slot_id((a, kind, "far"), 1)], second_core)
+            else:
+                for block in (0, 1):
+                    landed(dst(xs, block), x_sem(a, kind, xs, block), holders[a][1])
+            return
         for block in (0, 1):
             only = second_core if (xs, block) == (0, 0) else None
             landed(dst(xs, block), x_sem(a, kind, xs, block), only)
@@ -251,17 +263,14 @@
         for a, (_, buf) in enumerate(sources):
             buf[0, 0, 0, :, right] = own_right[a]
 
-    load_in.wait()
-    send_in = send(w_in.at[c], w_in.at[c], partner)
-    load_out.wait()
-    send_out = send(w_out.at[c], w_out.at[c], partner)
-
-    for k in range(chunks):
+    for k in turns:
         for a in (0, 1):
             for xs in range(k * per, (k + 1) * per):
                 from_x(a, "r", xs, right_at(a))
             for d in direct(hz, sides[a]):
                 rz[a, k, d] = send(right_block(a, k, 0), right_block(a, k, slot[-d]), to_z(d))
+    load_in.wait()
+    send_in = send(w_in.at[c], w_in.at[c], partner)
     for a in (0, 1):
         for sgn, d in relayed(hz, sides[a]):
             if d == 3:
@@ -273,7 +282,9 @@
             if not (hz > 2 and abs(d) == 2):
                 lz[a, d].wait_recv()
         over_x(a, 0, stage.at[a, batches[0]], left_at(a, batches[0]))
-    for k in range(chunks):
+    load_out.wait()
+    send_out = send(w_out.at[c], w_out.at[c], partner)
+    for k in turns:
         for a in (0, 1):
             for sgn, d in relayed(hz, sides[a]):
                 if d == 3:
@@ -288,11 +299,16 @@
             lz[a, d * sgn].wait_recv()
         if near < nz:
             over_x(a, 1, stage.at[a, batches[1]], left_at(a, batches[1]))
+        relay_x(a, 0, batches[0])
 
     @pl.when(first_core)
     def _():
         for a, (_, buf) in enumerate(sources):
             buf[0, 0, :, :, left] = stage[a]
+
+    if near < nz:
+        for a in (0, 1):
+            relay_x(a, 1, batches[1])
 
     def gathered(a, k):
         for d in direct(hz, sides[a]):
@@ -351,17 +367,17 @@
             value = value + ring_got(a, k, d)
         return value
 
-    for k in range(chunks):
+    for k in turns:
         for a in (0, 1):
             gathered(a, k)
-            if k == 0:
+            if k == turns[0]:
                 (send_in, send_out)[a].wait_recv()
             product(a, k)
             ring_first(a, k)
     shared = []
     for a, other in enumerate((tok_other, og_other)):
         shared.append(send(sources[a][1].at[:, 1 - c], other, partner))
-    for k in range(chunks):
+    for k in turns:
         ring_second(0, k)
         ring_second(1, k)
 
@@ -384,15 +400,15 @@
         for sgn, far in relayed(hy, sides[a]):
             spread[a, k, far * sgn].wait_recv()
 
-    for k in range(chunks):
+    for k in turns:
         preact = ring_end(0, k) + bias_in[...][None, None, :]
         act_all[c, spans[k], y] = gelu_value(preact).astype(BF16)
         slope = gelu_slope(preact)
         gp_all[c, spans[k], y] = (ring_end(1, k) * slope).astype(BF16)
         spread_first(gp_all, 1, k)
-    for k in range(chunks):
+    for k in turns:
         spread_second(gp_all, 1, k)
-    for k in range(chunks):
+    for k in turns:
         spread_first(act_all, 0, k)
 
     def row_terms(k, span):
@@ -508,7 +524,7 @@
             (((0,), (0,)), ((), ())),
             preferred_element_type=F32,
         )
-        gwi[span, :] = out.astype(BF16)
+        grad_weight_in[span, :] = out.astype(BF16)
 
     def weight_out_grad(i, n):
         step = hid // n
@@ -524,37 +540,35 @@
             (((0,), (0,)), ((), ())),
             preferred_element_type=F32,
         )
-        gwo[span, :] = out.astype(BF16)
-
-    for k in range(chunks):
+        grad_weight_out[span, :] = out.astype(BF16)
+
+    for k in turns:
         spread_end(1, k)
         row_terms(k, right)
         right_first(k)
         row_terms(k, left)
         home("left", k, lambda xs, block: g_send.at[xs, block, :, :, left], lx_in)
     shared.append(send(gp_all.at[c], gp_all.at[c], partner))
-    for k in range(chunks):
+    for k in turns:
         spread_second(act_all, 0, k)
-    for k in range(chunks):
+    for k in turns:
         right_second(k)
     left_first()
     for copy in shared:
         copy.wait_recv()
     weight_in_grad(0, 3)
-    for k in range(chunks):
+    for k in turns:
         spread_end(0, k)
     share_act = send(act_all.at[c], act_all.at[c], partner)
-    for k in range(chunks):
+    for k in turns:
         right_end(k)
     left_second()
     for i in (1, 2):
         weight_in_grad(i, 3)
-    store_in = local(gwi, grad_weight_in, 4)
-    grad_bias[...] = jnp.sum(gp_all[...].astype(F32).reshape(2 * half, hid), axis=0, keepdims=True)
+    grad_bias[...] = jnp.sum(gp_all[...].astype(F32).reshape(2 * half, hid), axis=0)
     share_act.wait_recv()
     for i in range(3):
         weight_out_grad(i, 3)
-    store_out = local(gwo, grad_weight_out, 5)
     left_end()
     at_home("right", rx_in)
 
@@ -566,8 +580,6 @@
     for s in range(1, nx):
         value = value + rx_in[s]
     grad_tokens[:, right] = value.astype(BF16)
-    store_in.wait()
-    store_out.wait()
     for copy, only in pending:
         if only is None:
             copy.wait_send()
@@ -589,13 +601,13 @@
     out = pl.pallas_call(
         functools.partial(kernel, nz, ny, chunks),
         out_shape=(
-            jax.ShapeDtypeStruct((rows, feat), BF16),
-            jax.ShapeDtypeStruct((feat, hid), BF16),
-            jax.ShapeDtypeStruct((hid, feat), BF16),
-            jax.ShapeDtypeStruct((1, hid), F32),
+            pltpu.VMEM((rows, feat), BF16),
+            pltpu.VMEM((feat, hid), BF16),
+            pltpu.VMEM((hid, feat), BF16),
+            pltpu.VMEM((hid,), F32),
         ),
         in_specs=[anywhere, anywhere, vmem, anywhere, anywhere],
-        out_specs=(vmem, anywhere, anywhere, vmem),
+        out_specs=(vmem, vmem, vmem, vmem),
         scratch_shapes=[
             pltpu.VMEM((nxs, 2, nz, rows, feat), BF16),
             pltpu.VMEM((nxs, 2, nz, rows, feat), BF16),
@@ -620,34 +632,23 @@
             pltpu.VMEM((chunks, nz - 1, per, 2, rows, rest), BF16),
             pltpu.VMEM((nxs, 2, rows, rest), F32),
             pltpu.VMEM((nx, rows, rest), F32),
-            pltpu.VMEM((feat, hid), BF16),
-            pltpu.VMEM((hid, feat), BF16),
             pltpu.SemaphoreType.DMA((N_SEMS,)),
             pltpu.SemaphoreType.DMA((N_SEMS,)),
             pltpu.SemaphoreType.DMA((64,)),
             pltpu.SemaphoreType.DMA((6,)),
         ],
         compiler_params=pltpu.CompilerParams(
-            collective_id=0, has_side_effects=True, vmem_limit_bytes=56 * 1024 * 1024
+            collective_id=0, has_side_effects=True, vmem_limit_bytes=LIMIT
         ),
     )(tokens, weight_in, bias_in, weight_out, out_grad)
     return pl.pallas_call(
         copy_out,
-        out_shape=(
-            jax.ShapeDtypeStruct((rows, feat), BF16),
-            jax.ShapeDtypeStruct((feat, hid), BF16),
-            jax.ShapeDtypeStruct((hid, feat), BF16),
-            jax.ShapeDtypeStruct((hid,), F32),
-        ),
-        in_specs=[vmem, anywhere, anywhere, vmem],
-        out_specs=(vmem, anywhere, anywhere, vmem),
-        scratch_shapes=[
-            pltpu.VMEM((feat, hid), BF16),
-            pltpu.VMEM((hid, feat), BF16),
-            pltpu.SemaphoreType.DMA((2, 3, 2)),
-        ],
-        compiler_params=pltpu.CompilerParams(vmem_limit_bytes=56 * 1024 * 1024),
-    )(*out)
+        out_shape=tuple(jax.ShapeDtypeStruct(v.shape, v.dtype) for v in out),
+        in_specs=[vmem] * 4,
+        out_specs=(anywhere,) * 4,
+        scratch_shapes=[pltpu.SemaphoreType.DMA((4,))],
+        compiler_params=pltpu.CompilerParams(vmem_limit_bytes=1024 * 1024),
+    )(*(pltpu.with_memory_space_constraint(v, pltpu.VMEM) for v in out))
 
 
 def solution(mesh):

time: 78.4 us -> 73.7 us (0.940)
  Pallas kernels: 77.5 us -> 72.9 us
    pallas_call x2, Pallas kernels: 77.5 us -> 72.9 us  [the longest x1 71.5 us: body(): pl.pallas_call(functools.partial(kernel, nz, ny, chunks), out_shape=(pltp...]
where the time goes in v4:
time: 73.7 us; the launch traced here: 73.6 us
  Pallas kernels  72.9 us (99%)
    pallas_call x1, Pallas kernels, body(): pl.pallas_call(functools.partial(kernel, nz, ny, chunks), out_shape=(pltp...  71.5 us

profile of v4, /device:TPU:1, one launch (start us, length us, event | category | flops | bytes accessed | tf_op | source)
XLA Modules:
  0.0 73.6 jit_solution(8045613897207233664)
XLA Ops:
  0.6 71.5 %shard_map.84 = (bf16[16,768]{1,0:T(8,128)(2,1)S(1)}, bf16[768,768]{1,0:T(8,128)(2,1)S(1)}, bf16[768,768]{1,0:T(8,128)(2,1)S(1)}, f32[768]{0:T(1024)S(1)}) custom-call(bf16[16,768]{1,0:T(8,128)(2,1)} %tokens.1, bf16[768,768]{1,0:T(8,128)(2,1)} %weight_in.1, f32[768]{0:T(1024)} %bias_in.1, bf16[768,768]{1,0:T(8,128)(2,1)} %weight_out.1, bf16[16,768]{1,0:T(8,128)(2,1)} %out_grad.1), custom_call_target="tpu_custom_call" | custom-call | tf_op jit(solution)/shard_map/pallas_call | solution.py:601
  72.1 1.4 %shard_map.85 = (bf16[16,768]{1,0:T(8,128)(2,1)}, bf16[768,768]{1,0:T(8,128)(2,1)}, bf16[768,768]{1,0:T(8,128)(2,1)}, f32[768]{0:T(1024)}) custom-call(bf16[16,768]{1,0:T(8,128)(2,1)S(1)} %get-tuple-element.8.refs_0_, bf16[768,768]{1,0:T(8,128)(2,1)S(1)} %get-tuple-element.9.refs_1_, bf16[768,768]{1,0:T(8,128)(2,1)S(1)} %get-tuple-element.10.refs_2_, ...), custom_call_target="tpu_custom_call" | custom-call | tf_op jit(solution)/shard_map/pallas_call | solution.py:644

commit v5 on v4

--- a/solution.py
+++ b/solution.py
@@ -194,7 +194,7 @@
         copy.wait()
 
     lz, rz = {}, {}
-    hops = sorted(range(1, nx), key=lambda j: (nx - j) % nxs)
+    hops = sorted(range(1, nx), key=lambda j: -((nx - j) % nxs))
 
     def far_relay(kind):
         return nx == 4 and kind != "r"
@@ -220,7 +220,7 @@
         return slot_sems.at[slot_id((a, kind, xs), 2) + block]
 
     def over_x(a, kind, src, dst):
-        for j in [0] + hops:
+        for j in hops + [0]:
             core, xs = divmod((nx - j) % nx, nxs)
             if far_relay(kind) and j == nx // 2:
                 continue
@@ -263,15 +263,25 @@
         for a, (_, buf) in enumerate(sources):
             buf[0, 0, 0, :, right] = own_right[a]
 
-    for k in turns:
+    def right_start(k):
         for a in (0, 1):
             for xs in range(k * per, (k + 1) * per):
                 from_x(a, "r", xs, right_at(a))
             for d in direct(hz, sides[a]):
                 rz[a, k, d] = send(right_block(a, k, 0), right_block(a, k, slot[-d]), to_z(d))
-    load_in.wait()
-    send_in = send(w_in.at[c], w_in.at[c], partner)
-    for a in (0, 1):
+
+    def right_relay(k):
+        for a in (0, 1):
+            for sgn, d in relayed(hz, sides[a]):
+                if d == 3:
+                    rz[a, k, 2 * sgn].wait_recv()
+                rz[a, k, d * sgn] = send(
+                    right_block(a, k, slot[-2 * sgn]),
+                    right_block(a, k, slot[-d * sgn]),
+                    to_z((d - 2) * sgn),
+                )
+
+    def left_relay(a):
         for sgn, d in relayed(hz, sides[a]):
             if d == 3:
                 lz[a, 2 * sgn].wait_recv()
@@ -282,33 +292,31 @@
             if not (hz > 2 and abs(d) == 2):
                 lz[a, d].wait_recv()
         over_x(a, 0, stage.at[a, batches[0]], left_at(a, batches[0]))
-    load_out.wait()
-    send_out = send(w_out.at[c], w_out.at[c], partner)
-    for k in turns:
-        for a in (0, 1):
-            for sgn, d in relayed(hz, sides[a]):
-                if d == 3:
-                    rz[a, k, 2 * sgn].wait_recv()
-                rz[a, k, d * sgn] = send(
-                    right_block(a, k, slot[-2 * sgn]),
-                    right_block(a, k, slot[-d * sgn]),
-                    to_z((d - 2) * sgn),
-                )
-    for a in (0, 1):
+
+    def left_rest(a):
         for sgn, d in relayed(hz, sides[a]):
             lz[a, d * sgn].wait_recv()
         if near < nz:
             over_x(a, 1, stage.at[a, batches[1]], left_at(a, batches[1]))
+
+    right_start(turns[0])
+    load_in.wait()
+    send_in = send(w_in.at[c], w_in.at[c], partner)
+    for a in (0, 1):
+        left_relay(a)
+    load_out.wait()
+    send_out = send(w_out.at[c], w_out.at[c], partner)
+    right_relay(turns[0])
+    for k in turns[1:]:
+        right_start(k)
+    for a in (0, 1):
+        left_rest(a)
         relay_x(a, 0, batches[0])
 
     @pl.when(first_core)
     def _():
         for a, (_, buf) in enumerate(sources):
             buf[0, 0, :, :, left] = stage[a]
-
-    if near < nz:
-        for a in (0, 1):
-            relay_x(a, 1, batches[1])
 
     def gathered(a, k):
         for d in direct(hz, sides[a]):
@@ -367,19 +375,23 @@
             value = value + ring_got(a, k, d)
         return value
 
-    for k in turns:
+    flushed = [0]
+
+    def flush():
+        for copy, only in pending[flushed[0] :]:
+            if only is None:
+                copy.wait_send()
+            else:
+                pl.when(only)(copy.wait_send)
+        flushed[0] = len(pending)
+
+    def multiply(k):
         for a in (0, 1):
             gathered(a, k)
             if k == turns[0]:
                 (send_in, send_out)[a].wait_recv()
             product(a, k)
             ring_first(a, k)
-    shared = []
-    for a, other in enumerate((tok_other, og_other)):
-        shared.append(send(sources[a][1].at[:, 1 - c], other, partner))
-    for k in turns:
-        ring_second(0, k)
-        ring_second(1, k)
 
     spread = {}
 
@@ -400,16 +412,12 @@
         for sgn, far in relayed(hy, sides[a]):
             spread[a, k, far * sgn].wait_recv()
 
-    for k in turns:
+    def pointwise(k):
         preact = ring_end(0, k) + bias_in[...][None, None, :]
         act_all[c, spans[k], y] = gelu_value(preact).astype(BF16)
         slope = gelu_slope(preact)
         gp_all[c, spans[k], y] = (ring_end(1, k) * slope).astype(BF16)
         spread_first(gp_all, 1, k)
-    for k in turns:
-        spread_second(gp_all, 1, k)
-    for k in turns:
-        spread_first(act_all, 0, k)
 
     def row_terms(k, span):
         grads = gp_all[c, spans[k]].reshape(per * nz * rows, hid)
@@ -542,31 +550,71 @@
         )
         grad_weight_out[span, :] = out.astype(BF16)
 
-    for k in turns:
+    shared = []
+
+    def row_start(k):
         spread_end(1, k)
         row_terms(k, right)
         right_first(k)
         row_terms(k, left)
         home("left", k, lambda xs, block: g_send.at[xs, block, :, :, left], lx_in)
-    shared.append(send(gp_all.at[c], gp_all.at[c], partner))
+        block = gp_all.at[c, spans[k]]
+        shared.append(send(block, block, partner))
+
+    def share_act(k):
+        spread_end(0, k)
+        block = act_all.at[c, spans[k]]
+        shared.append(send(block, block, partner))
+
+    one, rest_turns = turns[0], list(turns[1:])
+    for a in (0, 1):
+        if near < nz:
+            relay_x(a, 1, batches[1])
+    multiply(one)
+    for k in rest_turns:
+        right_relay(k)
+    ring_second(0, one)
+    ring_second(1, one)
+    for k in rest_turns:
+        multiply(k)
+    pointwise(one)
+    for a, other in enumerate((tok_other, og_other)):
+        shared.append(send(sources[a][1].at[:, 1 - c], other, partner))
+    for k in rest_turns:
+        ring_second(0, k)
+        ring_second(1, k)
+    spread_second(gp_all, 1, one)
+    for k in rest_turns:
+        pointwise(k)
+    row_start(one)
+    for k in rest_turns:
+        spread_second(gp_all, 1, k)
+    for k in turns:
+        spread_first(act_all, 0, k)
+    flush()
+    right_second(one)
+    for k in rest_turns:
+        row_start(k)
     for k in turns:
         spread_second(act_all, 0, k)
-    for k in turns:
+    for copy in shared:
+        copy.wait_recv()
+    shared.clear()
+    weight_in_grad(0, 3)
+    for k in rest_turns:
         right_second(k)
     left_first()
-    for copy in shared:
-        copy.wait_recv()
-    weight_in_grad(0, 3)
-    for k in turns:
-        spread_end(0, k)
-    share_act = send(act_all.at[c], act_all.at[c], partner)
+    weight_in_grad(1, 3)
     for k in turns:
         right_end(k)
     left_second()
-    for i in (1, 2):
-        weight_in_grad(i, 3)
+    for k in turns:
+        share_act(k)
+    weight_in_grad(2, 3)
     grad_bias[...] = jnp.sum(gp_all[...].astype(F32).reshape(2 * half, hid), axis=0)
-    share_act.wait_recv()
+    flush()
+    for copy in shared:
+        copy.wait_recv()
     for i in range(3):
         weight_out_grad(i, 3)
     left_end()
@@ -580,11 +628,7 @@
     for s in range(1, nx):
         value = value + rx_in[s]
     grad_tokens[:, right] = value.astype(BF16)
-    for copy, only in pending:
-        if only is None:
-            copy.wait_send()
-        else:
-            pl.when(only)(copy.wait_send)
+    flush()
 
 
 def body(nz, ny, tokens, weight_in, bias_in, weight_out, out_grad):

time: 73.7 us -> 72.1 us (0.978); the launches traced: 73.6 us -> 71 us
  Pallas kernels: 72.9 us -> 70.4 us
    pallas_call x1, Pallas kernels: 71.5 us -> 68.9 us  [body(): pl.pallas_call(functools.partial(kernel, nz, ny, chunks), out_shape=(pltp...]
where the time goes in v5:
time: 72.1 us; the launch traced here: 71 us
  Pallas kernels  70.4 us (98%)
    pallas_call x1, Pallas kernels, body(): pl.pallas_call(functools.partial(kernel, nz, ny, chunks), out_shape=(pltp...  68.9 us
    pallas_call x1, Pallas kernels, body(): pl.pallas_call(copy_out, out_shape=tuple((jax.ShapeDtypeStruct(v.shape, v...  1.44 us

profile of v5, /device:TPU:1, one launch (start us, length us, event | category | flops | bytes accessed | tf_op | source)
XLA Modules:
  0.0 71.0 jit_solution(10641682995080897334)
XLA Ops:
  0.6 68.9 %shard_map.84 = (bf16[16,768]{1,0:T(8,128)(2,1)S(1)}, bf16[768,768]{1,0:T(8,128)(2,1)S(1)}, bf16[768,768]{1,0:T(8,128)(2,1)S(1)}, f32[768]{0:T(1024)S(1)}) custom-call(bf16[16,768]{1,0:T(8,128)(2,1)} %tokens.1, bf16[768,768]{1,0:T(8,128)(2,1)} %weight_in.1, f32[768]{0:T(1024)} %bias_in.1, bf16[768,768]{1,0:T(8,128)(2,1)} %weight_out.1, bf16[16,768]{1,0:T(8,128)(2,1)} %out_grad.1), custom_call_target="tpu_custom_call" | custom-call | tf_op jit(solution)/shard_map/pallas_call | solution.py:645
  69.6 1.4 %shard_map.85 = (bf16[16,768]{1,0:T(8,128)(2,1)}, bf16[768,768]{1,0:T(8,128)(2,1)}, bf16[768,768]{1,0:T(8,128)(2,1)}, f32[768]{0:T(1024)}) custom-call(bf16[16,768]{1,0:T(8,128)(2,1)S(1)} %get-tuple-element.8.refs_0_, bf16[768,768]{1,0:T(8,128)(2,1)S(1)} %get-tuple-element.9.refs_1_, bf16[768,768]{1,0:T(8,128)(2,1)S(1)} %get-tuple-element.10.refs_2_, ...), custom_call_target="tpu_custom_call" | custom-call | tf_op jit(solution)/shard_map/pallas_call | solution.py:688

commit v6 on v5

--- a/solution.py
+++ b/solution.py
@@ -11,7 +11,7 @@
 INV_ROOT_TWO_PI = 0.3989422804014327
 X = 4
 N_SEMS = 192
-CHUNKS = 2
+CHUNKS = 1
 LIMIT = 56 * 1024 * 1024
 BF16, F32 = jnp.bfloat16, jnp.float32
 MESH = pl.DeviceIdType.MESH

time: 72.1 us -> 76.8 us (1.065); the launches traced: 71 us -> 76.6 us
  Pallas kernels: 70.4 us -> 76 us
    pallas_call x1, Pallas kernels: 68.9 us -> 74.6 us  [body(): pl.pallas_call(functools.partial(kernel, nz, ny, chunks), out_shape=(pltp...]
where the time goes in v6:
time: 76.8 us; the launch traced here: 76.6 us
  Pallas kernels  76 us (99%)
    pallas_call x1, Pallas kernels, body(): pl.pallas_call(functools.partial(kernel, nz, ny, chunks), out_shape=(pltp...  74.6 us

profile of v6, /device:TPU:1, one launch (start us, length us, event | category | flops | bytes accessed | tf_op | source)
XLA Modules:
  0.0 76.6 jit_solution(9505274303649470625)
XLA Ops:
  0.6 74.6 %shard_map.84 = (bf16[16,768]{1,0:T(8,128)(2,1)S(1)}, bf16[768,768]{1,0:T(8,128)(2,1)S(1)}, bf16[768,768]{1,0:T(8,128)(2,1)S(1)}, f32[768]{0:T(1024)S(1)}) custom-call(bf16[16,768]{1,0:T(8,128)(2,1)} %tokens.1, bf16[768,768]{1,0:T(8,128)(2,1)} %weight_in.1, f32[768]{0:T(1024)} %bias_in.1, bf16[768,768]{1,0:T(8,128)(2,1)} %weight_out.1, bf16[16,768]{1,0:T(8,128)(2,1)} %out_grad.1), custom_call_target="tpu_custom_call" | custom-call | tf_op jit(solution)/shard_map/pallas_call | solution.py:645
  75.2 1.4 %shard_map.85 = (bf16[16,768]{1,0:T(8,128)(2,1)}, bf16[768,768]{1,0:T(8,128)(2,1)}, bf16[768,768]{1,0:T(8,128)(2,1)}, f32[768]{0:T(1024)}) custom-call(bf16[16,768]{1,0:T(8,128)(2,1)S(1)} %get-tuple-element.8.refs_0_, bf16[768,768]{1,0:T(8,128)(2,1)S(1)} %get-tuple-element.9.refs_1_, bf16[768,768]{1,0:T(8,128)(2,1)S(1)} %get-tuple-element.10.refs_2_, ...), custom_call_target="tpu_custom_call" | custom-call | tf_op jit(solution)/shard_map/pallas_call | solution.py:688

commit v7 on v5

--- a/solution.py
+++ b/solution.py
@@ -59,6 +59,7 @@
     og_half,
     tok_other,
     og_other,
+    tok_t,
     stage,
     own_right,
     w_in,
@@ -157,6 +158,8 @@
         return copy
 
     left, right = pl.ds(0, cut), pl.ds(cut, rest)
+    low = lx_in.shape[-1]
+    west, east = pl.ds(0, low), pl.ds(low, feat - low)
     slot = {d: i for i, d in enumerate(around(nz))}
     slot[-hz] = slot[hz]
     near = 2 * min(hz, 3) - 1
@@ -455,14 +458,14 @@
     def right_first(k):
         for sgn, d in relayed(hz, 1):
             o = d * sgn
-            right_put(k, o, g_send.at[spans[k], :, slot[o], :, right], (d - 2) * sgn)
+            right_put(k, o, g_send.at[spans[k], :, slot[o], :, east], (d - 2) * sgn)
         for o in direct(hz, 1):
             if abs(o) == 1:
-                right_put(k, o, g_send.at[spans[k], :, slot[o], :, right], o)
+                right_put(k, o, g_send.at[spans[k], :, slot[o], :, east], o)
 
     def right_second(k):
         for i, o in enumerate(d for d in direct(hz, 1) if abs(d) == 2):
-            value = g_full[spans[k], :, slot[o], :, right]
+            value = g_full[spans[k], :, slot[o], :, east]
             for sgn, d in relayed(hz, 1):
                 if sgn * o > 0:
                     value = value + right_got(k, d * sgn)
@@ -470,7 +473,7 @@
             right_put(k, o, rz_out.at[k, i], o)
 
     def right_end(k):
-        value = g_full[spans[k], :, 0, :, right]
+        value = g_full[spans[k], :, 0, :, east]
         for o in reversed(direct(hz, 1)):
             value = value + right_got(k, o)
         rx_sum[spans[k]] = value
@@ -489,7 +492,7 @@
 
         @pl.when(first_core)
         def _():
-            lx_in[0] = g_send[0, 0, :, :, left]
+            lx_in[0] = g_send[0, 0, :, :, west]
 
         value = lx_in[0].astype(F32)
         for s in range(1, nx):
@@ -514,23 +517,17 @@
         value = lz_sum[0]
         for o in reversed(direct(hz, -1)):
             value = value + left_got(o)
-        grad_tokens[:, left] = value.astype(BF16)
+        grad_tokens[:, west] = value.astype(BF16)
 
     half = nxs * nz * rows
 
     def weight_in_grad(i, n):
         step = feat // n
         span = pl.ds(i * step, step)
-        out = lax.dot_general(
-            tok_half[:, c, :, :, span].reshape(half, step),
-            gp_all[c].reshape(half, hid),
-            (((0,), (0,)), ((), ())),
-            preferred_element_type=F32,
-        ) + lax.dot_general(
-            tok_other[:, :, :, span].reshape(half, step),
-            gp_all[1 - c].reshape(half, hid),
-            (((0,), (0,)), ((), ())),
-            preferred_element_type=F32,
+        out = jnp.dot(
+            tok_t[0, span], gp_all[c].reshape(half, hid), preferred_element_type=F32
+        ) + jnp.dot(
+            tok_t[1, span], gp_all[1 - c].reshape(half, hid), preferred_element_type=F32
         )
         grad_weight_in[span, :] = out.astype(BF16)
 
@@ -554,10 +551,10 @@
 
     def row_start(k):
         spread_end(1, k)
-        row_terms(k, right)
+        row_terms(k, east)
         right_first(k)
-        row_terms(k, left)
-        home("left", k, lambda xs, block: g_send.at[xs, block, :, :, left], lx_in)
+        row_terms(k, west)
+        home("left", k, lambda xs, block: g_send.at[xs, block, :, :, west], lx_in)
         block = gp_all.at[c, spans[k]]
         shared.append(send(block, block, partner))
 
@@ -565,6 +562,11 @@
         spread_end(0, k)
         block = act_all.at[c, spans[k]]
         shared.append(send(block, block, partner))
+
+    def all_shared():
+        for copy in shared:
+            copy.wait_recv()
+        shared.clear()
 
     one, rest_turns = turns[0], list(turns[1:])
     for a in (0, 1):
@@ -584,6 +586,7 @@
         ring_second(0, k)
         ring_second(1, k)
     spread_second(gp_all, 1, one)
+    tok_t[0] = tok_half[:, c].reshape(half, feat).T
     for k in rest_turns:
         pointwise(k)
     row_start(one)
@@ -591,30 +594,30 @@
         spread_second(gp_all, 1, k)
     for k in turns:
         spread_first(act_all, 0, k)
-    flush()
+    shared[0].wait_recv()
+    tok_t[1] = tok_other[...].reshape(half, feat).T
     right_second(one)
     for k in rest_turns:
         row_start(k)
     for k in turns:
         spread_second(act_all, 0, k)
-    for copy in shared:
+    flush()
+    for copy in shared[1:]:
         copy.wait_recv()
     shared.clear()
     weight_in_grad(0, 3)
     for k in rest_turns:
         right_second(k)
     left_first()
+    for k in turns:
+        share_act(k)
     weight_in_grad(1, 3)
+    weight_in_grad(2, 3)
     for k in turns:
         right_end(k)
     left_second()
-    for k in turns:
-        share_act(k)
-    weight_in_grad(2, 3)
     grad_bias[...] = jnp.sum(gp_all[...].astype(F32).reshape(2 * half, hid), axis=0)
-    flush()
-    for copy in shared:
-        copy.wait_recv()
+    all_shared()
     for i in range(3):
         weight_out_grad(i, 3)
     left_end()
@@ -627,7 +630,7 @@
     value = rx_in[0]
     for s in range(1, nx):
         value = value + rx_in[s]
-    grad_tokens[:, right] = value.astype(BF16)
+    grad_tokens[:, east] = value.astype(BF16)
     flush()
 
 
@@ -636,6 +639,8 @@
     hid = weight_in.shape[1]
     cut = feat // 3 * 2
     rest = feat - cut
+    low = feat // 3
+    high = feat - low
     nx = X
     nxs = nx // 2
     chunks = min(CHUNKS, nxs)
@@ -657,6 +662,7 @@
             pltpu.VMEM((nxs, 2, nz, rows, feat), BF16),
             pltpu.VMEM((nxs, nz, rows, feat), BF16),
             pltpu.VMEM((nxs, nz, rows, feat), BF16),
+            pltpu.VMEM((2, feat, nxs * nz * rows), BF16),
             pltpu.VMEM((2, nz, rows, cut), BF16),
             pltpu.VMEM((2, rows, rest), BF16),
             pltpu.VMEM((2, feat, hid), BF16),
@@ -668,14 +674,14 @@
             pltpu.VMEM((2, nxs, ny, pr, hid), BF16),
             pltpu.VMEM((nxs, 2, nz, rows, feat), F32),
             pltpu.VMEM((nxs, 2, nz, rows, feat), BF16),
-            pltpu.VMEM((nx, nz, rows, cut), BF16),
-            pltpu.VMEM((nz, rows, cut), F32),
-            pltpu.VMEM((2, rows, cut), F32),
-            pltpu.VMEM((nz - 1, rows, cut), F32),
-            pltpu.VMEM((chunks, 2, per, 2, rows, rest), BF16),
-            pltpu.VMEM((chunks, nz - 1, per, 2, rows, rest), BF16),
-            pltpu.VMEM((nxs, 2, rows, rest), F32),
-            pltpu.VMEM((nx, rows, rest), F32),
+            pltpu.VMEM((nx, nz, rows, low), BF16),
+            pltpu.VMEM((nz, rows, low), F32),
+            pltpu.VMEM((2, rows, low), F32),
+            pltpu.VMEM((nz - 1, rows, low), F32),
+            pltpu.VMEM((chunks, 2, per, 2, rows, high), BF16),
+            pltpu.VMEM((chunks, nz - 1, per, 2, rows, high), BF16),
+            pltpu.VMEM((nxs, 2, rows, high), F32),
+            pltpu.VMEM((nx, rows, high), F32),
             pltpu.SemaphoreType.DMA((N_SEMS,)),
             pltpu.SemaphoreType.DMA((N_SEMS,)),
             pltpu.SemaphoreType.DMA((64,)),

time: 72.1 us -> 72.8 us (level); the launches traced: 71 us -> 72.7 us
  Pallas kernels: 70.4 us -> 72.1 us
    pallas_call x1, Pallas kernels: 68.9 us -> 70.6 us  [body(): pl.pallas_call(functools.partial(kernel, nz, ny, chunks), out_shape=(pltp...]
where the time goes in v7:
time: 72.8 us; the launch traced here: 72.7 us
  Pallas kernels  72.1 us (99%)
    pallas_call x1, Pallas kernels, body(): pl.pallas_call(functools.partial(kernel, nz, ny, chunks), out_shape=(pltp...  70.6 us

profile of v7, /device:TPU:1, one launch (start us, length us, event | category | flops | bytes accessed | tf_op | source)
XLA Modules:
  0.0 72.7 jit_solution(11803988418653420207)
XLA Ops:
  0.6 70.6 %shard_map.84 = (bf16[16,768]{1,0:T(8,128)(2,1)S(1)}, bf16[768,768]{1,0:T(8,128)(2,1)S(1)}, bf16[768,768]{1,0:T(8,128)(2,1)S(1)}, f32[768]{0:T(1024)S(1)}) custom-call(bf16[16,768]{1,0:T(8,128)(2,1)} %tokens.1, bf16[768,768]{1,0:T(8,128)(2,1)} %weight_in.1, f32[768]{0:T(1024)} %bias_in.1, bf16[768,768]{1,0:T(8,128)(2,1)} %weight_out.1, bf16[16,768]{1,0:T(8,128)(2,1)} %out_grad.1), custom_call_target="tpu_custom_call" | custom-call | tf_op jit(solution)/shard_map/pallas_call | solution.py:650
  71.3 1.4 %shard_map.85 = (bf16[16,768]{1,0:T(8,128)(2,1)}, bf16[768,768]{1,0:T(8,128)(2,1)}, bf16[768,768]{1,0:T(8,128)(2,1)}, f32[768]{0:T(1024)}) custom-call(bf16[16,768]{1,0:T(8,128)(2,1)S(1)} %get-tuple-element.8.refs_0_, bf16[768,768]{1,0:T(8,128)(2,1)S(1)} %get-tuple-element.9.refs_1_, bf16[768,768]{1,0:T(8,128)(2,1)S(1)} %get-tuple-element.10.refs_2_, ...), custom_call_target="tpu_custom_call" | custom-call | tf_op jit(solution)/shard_map/pallas_call | solution.py:694

commit v8 on v7

--- a/solution.py
+++ b/solution.py
@@ -331,18 +331,32 @@
             for i, zs in enumerate(batches):
                 from_x(a, i, xs, left_at(a, zs))
 
+    def tiles(extent, width=256):
+        width = min(width, extent)
+
+        def run(f):
+            def step(i, carry):
+                f(pl.ds(pl.multiple_of(i * width, width), width))
+                return carry
+
+            lax.fori_loop(0, extent // width, step, 0)
+
+        return run
+
     def product(a, k):
-        total = 0
-        for block in (0, 1):
-            lhs = sources[a][1][spans[k], block].reshape(per * nz * rows, feat)
-            if a == 0:
-                out = jnp.dot(lhs, w_in[block], preferred_element_type=F32)
-            else:
-                out = lax.dot_general(
-                    lhs, w_out[block], (((1,), (1,)), ((), ())), preferred_element_type=F32
-                )
-            total = out if block == 0 else total + out
-        part[a, spans[k]] = total.reshape(per, ny, pr, hid)
+        @tiles(hid)
+        def _(span):
+            total = 0
+            for block in (0, 1):
+                lhs = sources[a][1][spans[k], block].reshape(per * nz * rows, feat)
+                if a == 0:
+                    out = jnp.dot(lhs, w_in[block, :, span], preferred_element_type=F32)
+                else:
+                    out = lax.dot_general(
+                        lhs, w_out[block, span, :], (((1,), (1,)), ((), ())), preferred_element_type=F32
+                    )
+                total = out if block == 0 else total + out
+            part[a, spans[k], :, :, span] = total.reshape(per, ny, pr, span.size)
 
     ring = {}
 
@@ -422,14 +436,19 @@
         gp_all[c, spans[k], y] = (ring_end(1, k) * slope).astype(BF16)
         spread_first(gp_all, 1, k)
 
-    def row_terms(k, span):
-        grads = gp_all[c, spans[k]].reshape(per * nz * rows, hid)
-        for block in (0, 1):
+    def row_terms(k, start, extent):
+        def step(i, carry):
+            block = lax.rem(i, 2)
+            span = pl.ds(pl.multiple_of(start + lax.div(i, 2) * low, low), low)
+            grads = gp_all[c, spans[k]].reshape(per * nz * rows, hid)
             out = lax.dot_general(
                 grads, w_in[block, span, :], (((1,), (1,)), ((), ())), preferred_element_type=F32
-            ).reshape(per, nz, rows, span.size)
+            ).reshape(per, nz, rows, low)
             g_full[spans[k], block, :, :, span] = out
             g_send[spans[k], block, :, :, span] = out.astype(BF16)
+            return carry
+
+        lax.fori_loop(0, 2 * (extent // low), step, 0)
 
     tl, tr = {}, {}
 
@@ -523,37 +542,49 @@
 
     def weight_in_grad(i, n):
         step = feat // n
-        span = pl.ds(i * step, step)
-        out = jnp.dot(
-            tok_t[0, span], gp_all[c].reshape(half, hid), preferred_element_type=F32
-        ) + jnp.dot(
-            tok_t[1, span], gp_all[1 - c].reshape(half, hid), preferred_element_type=F32
-        )
-        grad_weight_in[span, :] = out.astype(BF16)
-
-    def weight_out_grad(i, n):
-        step = hid // n
-        span = pl.ds(i * step, step)
-        out = lax.dot_general(
-            act_all[c, :, :, :, span].reshape(half, step),
-            og_half[:, c].reshape(half, feat),
-            (((0,), (0,)), ((), ())),
-            preferred_element_type=F32,
-        ) + lax.dot_general(
-            act_all[1 - c, :, :, :, span].reshape(half, step),
-            og_other[...].reshape(half, feat),
-            (((0,), (0,)), ((), ())),
-            preferred_element_type=F32,
-        )
-        grad_weight_out[span, :] = out.astype(BF16)
+        rows_out = pl.ds(i * step, step)
+
+        @tiles(hid)
+        def _(span):
+            out = jnp.dot(
+                tok_t[0, rows_out],
+                gp_all[c, :, :, :, span].reshape(half, span.size),
+                preferred_element_type=F32,
+            ) + jnp.dot(
+                tok_t[1, rows_out],
+                gp_all[1 - c, :, :, :, span].reshape(half, span.size),
+                preferred_element_type=F32,
+            )
+            grad_weight_in[rows_out, span] = out.astype(BF16)
+
+    def weight_out_grad():
+        @tiles(hid)
+        def _(span):
+            out = lax.dot_general(
+                act_all[c, :, :, :, span].reshape(half, span.size),
+                og_half[:, c].reshape(half, feat),
+                (((0,), (0,)), ((), ())),
+                preferred_element_type=F32,
+            ) + lax.dot_general(
+                act_all[1 - c, :, :, :, span].reshape(half, span.size),
+                og_other[...].reshape(half, feat),
+                (((0,), (0,)), ((), ())),
+                preferred_element_type=F32,
+            )
+            grad_weight_out[span, :] = out.astype(BF16)
+
+    def turn(i, src):
+        @tiles(feat)
+        def _(span):
+            tok_t[i, span, :] = src(span).reshape(half, span.size).T
 
     shared = []
 
     def row_start(k):
         spread_end(1, k)
-        row_terms(k, east)
+        row_terms(k, low, feat - low)
         right_first(k)
-        row_terms(k, west)
+        row_terms(k, 0, low)
         home("left", k, lambda xs, block: g_send.at[xs, block, :, :, west], lx_in)
         block = gp_all.at[c, spans[k]]
         shared.append(send(block, block, partner))
@@ -586,7 +617,7 @@
         ring_second(0, k)
         ring_second(1, k)
     spread_second(gp_all, 1, one)
-    tok_t[0] = tok_half[:, c].reshape(half, feat).T
+    turn(0, lambda span: tok_half[:, c, :, :, span])
     for k in rest_turns:
         pointwise(k)
     row_start(one)
@@ -595,7 +626,7 @@
     for k in turns:
         spread_first(act_all, 0, k)
     shared[0].wait_recv()
-    tok_t[1] = tok_other[...].reshape(half, feat).T
+    turn(1, lambda span: tok_other[:, :, :, span])
     right_second(one)
     for k in rest_turns:
         row_start(k)
@@ -618,8 +649,7 @@
     left_second()
     grad_bias[...] = jnp.sum(gp_all[...].astype(F32).reshape(2 * half, hid), axis=0)
     all_shared()
-    for i in range(3):
-        weight_out_grad(i, 3)
+    weight_out_grad()
     left_end()
     at_home("right", rx_in)
 

time: 72.8 us -> 73.6 us (1.011)
    pallas_call x1, Pallas kernels: 70.6 us -> 71.4 us  [body(): pl.pallas_call(functools.partial(kernel, nz, ny, chunks), out_shape=(pltp...]
where the time goes in v8:
time: 73.6 us; the launch traced here: 73.5 us
  Pallas kernels  72.8 us (99%)
    pallas_call x1, Pallas kernels, body(): pl.pallas_call(functools.partial(kernel, nz, ny, chunks), out_shape=(pltp...  71.4 us

profile of v8, /device:TPU:1, one launch (start us, length us, event | category | flops | bytes accessed | tf_op | source)
XLA Modules:
  0.0 73.5 jit_solution(4611455960329283473)
XLA Ops:
  0.6 71.4 %shard_map.84 = (bf16[16,768]{1,0:T(8,128)(2,1)S(1)}, bf16[768,768]{1,0:T(8,128)(2,1)S(1)}, bf16[768,768]{1,0:T(8,128)(2,1)S(1)}, f32[768]{0:T(1024)S(1)}) custom-call(bf16[16,768]{1,0:T(8,128)(2,1)} %tokens.1, bf16[768,768]{1,0:T(8,128)(2,1)} %weight_in.1, f32[768]{0:T(1024)} %bias_in.1, bf16[768,768]{1,0:T(8,128)(2,1)} %weight_out.1, bf16[16,768]{1,0:T(8,128)(2,1)} %out_grad.1), custom_call_target="tpu_custom_call" | custom-call | tf_op jit(solution)/shard_map/pallas_call | solution.py:680
  72.0 1.4 %shard_map.85 = (bf16[16,768]{1,0:T(8,128)(2,1)}, bf16[768,768]{1,0:T(8,128)(2,1)}, bf16[768,768]{1,0:T(8,128)(2,1)}, f32[768]{0:T(1024)}) custom-call(bf16[16,768]{1,0:T(8,128)(2,1)S(1)} %get-tuple-element.8.refs_0_, bf16[768,768]{1,0:T(8,128)(2,1)S(1)} %get-tuple-element.9.refs_1_, bf16[768,768]{1,0:T(8,128)(2,1)S(1)} %get-tuple-element.10.refs_2_, ...), custom_call_target="tpu_custom_call" | custom-call | tf_op jit(solution)/shard_map/pallas_call | solution.py:724

commit v9 on v5

--- a/solution.py
+++ b/solution.py
@@ -55,8 +55,7 @@
     grad_weight_in,
     grad_weight_out,
     grad_bias,
-    tok_half,
-    og_half,
+    both,
     tok_other,
     og_other,
     stage,
@@ -174,6 +173,7 @@
     def relayed(h, side):
         return [(sgn, d) for sgn in (1, -1) for d in (3, 4) if d < h or (d == h and sgn == side)]
 
+    tok_half, og_half = both.at[0], both.at[1]
     sources = ((tokens, tok_half), (out_grad, og_half))
     sides = (1, -1)
     own = []
@@ -199,64 +199,64 @@
     def far_relay(kind):
         return nx == 4 and kind != "r"
 
-    holders = ((second_core, first_core), (first_core, second_core))
-
-    def relay_x(a, kind, zs):
-        if not far_relay(kind):
-            return
-        buf = sources[a][1]
-        holder = holders[a][0]
-        for block in (0, 1):
-            landed(buf.at[1, block, zs, :, left], x_sem(a, kind, 1, block), holder)
-        send(
-            buf.at[1, :, zs, :, left],
-            buf.at[0, :, zs, :, left],
-            to_x(1 if a == 0 else nx - 1, 1),
-            slot_sems.at[slot_id((a, kind, "far"), 1)],
-            holder,
-        )
-
-    def x_sem(a, kind, xs, block):
-        return slot_sems.at[slot_id((a, kind, xs), 2) + block]
-
-    def over_x(a, kind, src, dst):
+    def x_sem(kind, xs, block):
+        return slot_sems.at[slot_id((kind, xs), 2) + block]
+
+    def over_x(kind, src, dst):
         for j in hops + [0]:
             core, xs = divmod((nx - j) % nx, nxs)
             if far_relay(kind) and j == nx // 2:
                 continue
             if j == 0:
-                send(src, dst(0, 1), partner, x_sem(a, kind, 0, 1), second_core)
+                send(src, dst(0, 1), partner, x_sem(kind, 0, 1), second_core)
             else:
-                send(src, dst(xs, c), to_x(j, core), x_sem(a, kind, xs, c))
-
-    def from_x(a, kind, xs, dst):
-        if far_relay(kind):
-            if xs == 0:
-                landed(dst(0, 1), x_sem(a, kind, 0, 1), first_core)
-                landed(dst(0, slice(None)), slot_sems.at[slot_id((a, kind, "far"), 1)], second_core)
-            else:
-                for block in (0, 1):
-                    landed(dst(xs, block), x_sem(a, kind, xs, block), holders[a][1])
+                send(src, dst(xs, c), to_x(j, core), x_sem(kind, xs, c))
+
+    def from_x(kind, xs, dst):
+        for block in (0, 1):
+            only = second_core if (xs, block) == (0, 0) else None
+            landed(dst(xs, block), x_sem(kind, xs, block), only)
+
+    def left_at(zs):
+        return lambda xs, block: both.at[:, xs, block, zs, :, left]
+
+    def right_at(xs, block):
+        return both.at[:, xs, block, 0, :, right]
+
+    def relay_x(kind, zs):
+        if not far_relay(kind):
             return
         for block in (0, 1):
-            only = second_core if (xs, block) == (0, 0) else None
-            landed(dst(xs, block), x_sem(a, kind, xs, block), only)
-
-    def right_at(a):
-        buf = sources[a][1]
-        return lambda xs, block: buf.at[xs, block, 0, :, right]
-
-    def left_at(a, zs):
-        buf = sources[a][1]
-        return lambda xs, block: buf.at[xs, block, zs, :, left]
-
-    def right_block(a, k, s):
-        return sources[a][1].at[spans[k], :, s, :, right]
-
-    for a in (0, 1):
-        over_x(a, "r", own_right.at[a], right_at(a))
-        for d in direct(hz, sides[a]):
-            lz[a, d] = send(stage.at[a, 0], stage.at[a, slot[-d]], to_z(d))
+            landed(left_at(zs)(1, block), x_sem(kind, 1, block))
+        a = 1 - c
+        send(
+            both.at[a, 1, :, zs, :, left],
+            both.at[a, 0, :, zs, :, left],
+            to_x(c + (nx - 1) * (1 - c), 1),
+            slot_sems.at[slot_id((kind, "far"), 2) + a],
+        )
+
+    def from_x_left(kind, zs, xs):
+        if not far_relay(kind):
+            from_x(kind, xs, left_at(zs))
+        elif xs == 0:
+            landed(left_at(zs)(0, 1), x_sem(kind, 0, 1), first_core)
+            for a in (0, 1):
+                sem = slot_sems.at[slot_id((kind, "far"), 2) + a]
+                landed(both.at[a, 0, :, zs, :, left], sem, second_core)
+
+    far_side = [(sgn, hz, a) for a, sgn in enumerate(sides)] if hz > 2 else []
+    relays = [(1, 3, None), (-1, 3, None)] * (hz > 3) + far_side
+
+    def right_block(k, s, a=None):
+        return both.at[slice(None) if a is None else a, spans[k], :, s, :, right]
+
+    def stage_block(s, a=None):
+        return stage.at[slice(None) if a is None else a, s]
+
+    over_x("r", own_right, right_at)
+    for d in direct(hz, 1):
+        lz[d] = send(stage_block(0), stage_block(slot[-d]), to_z(d))
 
     @pl.when(first_core)
     def _():
@@ -264,69 +264,63 @@
             buf[0, 0, 0, :, right] = own_right[a]
 
     def right_start(k):
-        for a in (0, 1):
-            for xs in range(k * per, (k + 1) * per):
-                from_x(a, "r", xs, right_at(a))
-            for d in direct(hz, sides[a]):
-                rz[a, k, d] = send(right_block(a, k, 0), right_block(a, k, slot[-d]), to_z(d))
+        for xs in range(k * per, (k + 1) * per):
+            from_x("r", xs, right_at)
+        for d in direct(hz, 1):
+            rz[k, d] = send(right_block(k, 0), right_block(k, slot[-d]), to_z(d))
 
     def right_relay(k):
-        for a in (0, 1):
-            for sgn, d in relayed(hz, sides[a]):
-                if d == 3:
-                    rz[a, k, 2 * sgn].wait_recv()
-                rz[a, k, d * sgn] = send(
-                    right_block(a, k, slot[-2 * sgn]),
-                    right_block(a, k, slot[-d * sgn]),
-                    to_z((d - 2) * sgn),
-                )
-
-    def left_relay(a):
-        for sgn, d in relayed(hz, sides[a]):
+        for sgn, d, a in relays:
             if d == 3:
-                lz[a, 2 * sgn].wait_recv()
-            lz[a, d * sgn] = send(
-                stage.at[a, slot[-2 * sgn]], stage.at[a, slot[-d * sgn]], to_z((d - 2) * sgn)
+                rz[k, 2 * sgn].wait_recv()
+            rz[k, d * sgn, a] = send(
+                right_block(k, slot[-2 * sgn], a), right_block(k, slot[-d * sgn], a), to_z((d - 2) * sgn)
             )
-        for d in direct(hz, sides[a]):
+
+    def left_relay():
+        for sgn, d, a in relays:
+            if d == 3:
+                lz[2 * sgn].wait_recv()
+            lz[d * sgn, a] = send(
+                stage_block(slot[-2 * sgn], a), stage_block(slot[-d * sgn], a), to_z((d - 2) * sgn)
+            )
+        for d in direct(hz, 1):
             if not (hz > 2 and abs(d) == 2):
-                lz[a, d].wait_recv()
-        over_x(a, 0, stage.at[a, batches[0]], left_at(a, batches[0]))
-
-    def left_rest(a):
-        for sgn, d in relayed(hz, sides[a]):
-            lz[a, d * sgn].wait_recv()
+                lz[d].wait_recv()
+        over_x(0, stage.at[:, batches[0]], left_at(batches[0]))
+
+    def left_rest():
+        for sgn, d, a in relays:
+            lz[d * sgn, a].wait_recv()
         if near < nz:
-            over_x(a, 1, stage.at[a, batches[1]], left_at(a, batches[1]))
+            over_x(1, stage.at[:, batches[1]], left_at(batches[1]))
 
     right_start(turns[0])
     load_in.wait()
     send_in = send(w_in.at[c], w_in.at[c], partner)
-    for a in (0, 1):
-        left_relay(a)
+    left_relay()
     load_out.wait()
     send_out = send(w_out.at[c], w_out.at[c], partner)
     right_relay(turns[0])
     for k in turns[1:]:
         right_start(k)
-    for a in (0, 1):
-        left_rest(a)
-        relay_x(a, 0, batches[0])
+    left_rest()
+    relay_x(0, batches[0])
 
     @pl.when(first_core)
     def _():
         for a, (_, buf) in enumerate(sources):
             buf[0, 0, :, :, left] = stage[a]
 
-    def gathered(a, k):
-        for d in direct(hz, sides[a]):
+    def gathered(k):
+        for d in direct(hz, 1):
             if not (hz > 2 and abs(d) == 2):
-                rz[a, k, d].wait_recv()
-        for sgn, d in relayed(hz, sides[a]):
-            rz[a, k, d * sgn].wait_recv()
+                rz[k, d].wait_recv()
+        for sgn, d, a in relays:
+            rz[k, d * sgn, a].wait_recv()
         for xs in range(k * per, (k + 1) * per):
             for i, zs in enumerate(batches):
-                from_x(a, i, xs, left_at(a, zs))
+                from_x_left(i, zs, xs)
 
     def product(a, k):
         total = 0
@@ -386,8 +380,8 @@
         flushed[0] = len(pending)
 
     def multiply(k):
+        gathered(k)
         for a in (0, 1):
-            gathered(a, k)
             if k == turns[0]:
                 (send_in, send_out)[a].wait_recv()
             product(a, k)
@@ -567,9 +561,8 @@
         shared.append(send(block, block, partner))
 
     one, rest_turns = turns[0], list(turns[1:])
-    for a in (0, 1):
-        if near < nz:
-            relay_x(a, 1, batches[1])
+    if near < nz:
+        relay_x(1, batches[1])
     multiply(one)
     for k in rest_turns:
         right_relay(k)
@@ -653,8 +646,7 @@
         in_specs=[anywhere, anywhere, vmem, anywhere, anywhere],
         out_specs=(vmem, vmem, vmem, vmem),
         scratch_shapes=[
-            pltpu.VMEM((nxs, 2, nz, rows, feat), BF16),
-            pltpu.VMEM((nxs, 2, nz, rows, feat), BF16),
+            pltpu.VMEM((2, nxs, 2, nz, rows, feat), BF16),
             pltpu.VMEM((nxs, nz, rows, feat), BF16),
             pltpu.VMEM((nxs, nz, rows, feat), BF16),
             pltpu.VMEM((2, nz, rows, cut), BF16),

time: 72.1 us -> 71.9 us (level); the launches traced: 71 us -> 71.7 us
  no operation moved by 1% of the time
where the time goes in v9:
time: 71.9 us; the launch traced here: 71.7 us
  Pallas kernels  71.1 us (99%)
    pallas_call x1, Pallas kernels, body(): pl.pallas_call(functools.partial(kernel, nz, ny, chunks), out_shape=(pltp...  69.6 us
    pallas_call x1, Pallas kernels, body(): pl.pallas_call(copy_out, out_shape=tuple((jax.ShapeDtypeStruct(v.shape, v...  1.44 us

profile of v9, /device:TPU:1, one launch (start us, length us, event | category | flops | bytes accessed | tf_op | source)
XLA Modules:
  0.0 71.7 jit_solution(7144660866561388142)
XLA Ops:
  0.6 69.6 %shard_map.84 = (bf16[16,768]{1,0:T(8,128)(2,1)S(1)}, bf16[768,768]{1,0:T(8,128)(2,1)S(1)}, bf16[768,768]{1,0:T(8,128)(2,1)S(1)}, f32[768]{0:T(1024)S(1)}) custom-call(bf16[16,768]{1,0:T(8,128)(2,1)} %tokens.1, bf16[768,768]{1,0:T(8,128)(2,1)} %weight_in.1, f32[768]{0:T(1024)} %bias_in.1, bf16[768,768]{1,0:T(8,128)(2,1)} %weight_out.1, bf16[16,768]{1,0:T(8,128)(2,1)} %out_grad.1), custom_call_target="tpu_custom_call" | custom-call | tf_op jit(solution)/shard_map/pallas_call | solution.py:638
  70.3 1.4 %shard_map.85 = (bf16[16,768]{1,0:T(8,128)(2,1)}, bf16[768,768]{1,0:T(8,128)(2,1)}, bf16[768,768]{1,0:T(8,128)(2,1)}, f32[768]{0:T(1024)}) custom-call(bf16[16,768]{1,0:T(8,128)(2,1)S(1)} %get-tuple-element.8.refs_0_, bf16[768,768]{1,0:T(8,128)(2,1)S(1)} %get-tuple-element.9.refs_1_, bf16[768,768]{1,0:T(8,128)(2,1)S(1)} %get-tuple-element.10.refs_2_, ...), custom_call_target="tpu_custom_call" | custom-call | tf_op jit(solution)/shard_map/pallas_call | solution.py:680

commit v10 on v9

--- a/solution.py
+++ b/solution.py
@@ -584,10 +584,10 @@
         spread_second(gp_all, 1, k)
     for k in turns:
         spread_first(act_all, 0, k)
-    flush()
-    right_second(one)
     for k in rest_turns:
         row_start(k)
+    right_second(one)
+    flush()
     for k in turns:
         spread_second(act_all, 0, k)
     for copy in shared:
@@ -597,12 +597,12 @@
     for k in rest_turns:
         right_second(k)
     left_first()
+    for k in turns:
+        share_act(k)
     weight_in_grad(1, 3)
     for k in turns:
         right_end(k)
     left_second()
-    for k in turns:
-        share_act(k)
     weight_in_grad(2, 3)
     grad_bias[...] = jnp.sum(gp_all[...].astype(F32).reshape(2 * half, hid), axis=0)
     flush()

time: 71.9 us -> 73.2 us (1.018)
  Pallas kernels: 71.1 us -> 72.4 us
    pallas_call x1, Pallas kernels: 69.6 us -> 71 us  [body(): pl.pallas_call(functools.partial(kernel, nz, ny, chunks), out_shape=(pltp...]
where the time goes in v10:
time: 73.2 us; the launch traced here: 73.1 us
  Pallas kernels  72.4 us (99%)
    pallas_call x1, Pallas kernels, body(): pl.pallas_call(functools.partial(kernel, nz, ny, chunks), out_shape=(pltp...  71 us

profile of v10, /device:TPU:1, one launch (start us, length us, event | category | flops | bytes accessed | tf_op | source)
XLA Modules:
  0.0 73.1 jit_solution(12146085342733176745)
XLA Ops:
  0.6 71.0 %shard_map.84 = (bf16[16,768]{1,0:T(8,128)(2,1)S(1)}, bf16[768,768]{1,0:T(8,128)(2,1)S(1)}, bf16[768,768]{1,0:T(8,128)(2,1)S(1)}, f32[768]{0:T(1024)S(1)}) custom-call(bf16[16,768]{1,0:T(8,128)(2,1)} %tokens.1, bf16[768,768]{1,0:T(8,128)(2,1)} %weight_in.1, f32[768]{0:T(1024)} %bias_in.1, bf16[768,768]{1,0:T(8,128)(2,1)} %weight_out.1, bf16[16,768]{1,0:T(8,128)(2,1)} %out_grad.1), custom_call_target="tpu_custom_call" | custom-call | tf_op jit(solution)/shard_map/pallas_call | solution.py:638
  71.6 1.4 %shard_map.85 = (bf16[16,768]{1,0:T(8,128)(2,1)}, bf16[768,768]{1,0:T(8,128)(2,1)}, bf16[768,768]{1,0:T(8,128)(2,1)}, f32[768]{0:T(1024)}) custom-call(bf16[16,768]{1,0:T(8,128)(2,1)S(1)} %get-tuple-element.8.refs_0_, bf16[768,768]{1,0:T(8,128)(2,1)S(1)} %get-tuple-element.9.refs_1_, bf16[768,768]{1,0:T(8,128)(2,1)S(1)} %get-tuple-element.10.refs_2_, ...), custom_call_target="tpu_custom_call" | custom-call | tf_op jit(solution)/shard_map/pallas_call | solution.py:680

commit v11 on v9

--- a/solution.py
+++ b/solution.py
@@ -156,6 +156,8 @@
         return copy
 
     left, right = pl.ds(0, cut), pl.ds(cut, rest)
+    low = lx_in.shape[-1]
+    west, east = pl.ds(0, low), pl.ds(low, feat - low)
     slot = {d: i for i, d in enumerate(around(nz))}
     slot[-hz] = slot[hz]
     near = 2 * min(hz, 3) - 1
@@ -449,14 +451,14 @@
     def right_first(k):
         for sgn, d in relayed(hz, 1):
             o = d * sgn
-            right_put(k, o, g_send.at[spans[k], :, slot[o], :, right], (d - 2) * sgn)
+            right_put(k, o, g_send.at[spans[k], :, slot[o], :, east], (d - 2) * sgn)
         for o in direct(hz, 1):
             if abs(o) == 1:
-                right_put(k, o, g_send.at[spans[k], :, slot[o], :, right], o)
+                right_put(k, o, g_send.at[spans[k], :, slot[o], :, east], o)
 
     def right_second(k):
         for i, o in enumerate(d for d in direct(hz, 1) if abs(d) == 2):
-            value = g_full[spans[k], :, slot[o], :, right]
+            value = g_full[spans[k], :, slot[o], :, east]
             for sgn, d in relayed(hz, 1):
                 if sgn * o > 0:
                     value = value + right_got(k, d * sgn)
@@ -464,7 +466,7 @@
             right_put(k, o, rz_out.at[k, i], o)
 
     def right_end(k):
-        value = g_full[spans[k], :, 0, :, right]
+        value = g_full[spans[k], :, 0, :, east]
         for o in reversed(direct(hz, 1)):
             value = value + right_got(k, o)
         rx_sum[spans[k]] = value
@@ -483,7 +485,7 @@
 
         @pl.when(first_core)
         def _():
-            lx_in[0] = g_send[0, 0, :, :, left]
+            lx_in[0] = g_send[0, 0, :, :, west]
 
         value = lx_in[0].astype(F32)
         for s in range(1, nx):
@@ -508,7 +510,7 @@
         value = lz_sum[0]
         for o in reversed(direct(hz, -1)):
             value = value + left_got(o)
-        grad_tokens[:, left] = value.astype(BF16)
+        grad_tokens[:, west] = value.astype(BF16)
 
     half = nxs * nz * rows
 
@@ -548,10 +550,10 @@
 
     def row_start(k):
         spread_end(1, k)
-        row_terms(k, right)
+        row_terms(k, east)
         right_first(k)
-        row_terms(k, left)
-        home("left", k, lambda xs, block: g_send.at[xs, block, :, :, left], lx_in)
+        row_terms(k, west)
+        home("left", k, lambda xs, block: g_send.at[xs, block, :, :, west], lx_in)
         block = gp_all.at[c, spans[k]]
         shared.append(send(block, block, partner))
 
@@ -620,7 +622,7 @@
     value = rx_in[0]
     for s in range(1, nx):
         value = value + rx_in[s]
-    grad_tokens[:, right] = value.astype(BF16)
+    grad_tokens[:, east] = value.astype(BF16)
     flush()
 
 
@@ -629,6 +631,8 @@
     hid = weight_in.shape[1]
     cut = feat // 3 * 2
     rest = feat - cut
+    low = feat // 3
+    high = feat - low
     nx = X
     nxs = nx // 2
     chunks = min(CHUNKS, nxs)
@@ -660,14 +664,14 @@
             pltpu.VMEM((2, nxs, ny, pr, hid), BF16),
             pltpu.VMEM((nxs, 2, nz, rows, feat), F32),
             pltpu.VMEM((nxs, 2, nz, rows, feat), BF16),
-            pltpu.VMEM((nx, nz, rows, cut), BF16),
-            pltpu.VMEM((nz, rows, cut), F32),
-            pltpu.VMEM((2, rows, cut), F32),
-            pltpu.VMEM((nz - 1, rows, cut), F32),
-            pltpu.VMEM((chunks, 2, per, 2, rows, rest), BF16),
-            pltpu.VMEM((chunks, nz - 1, per, 2, rows, rest), BF16),
-            pltpu.VMEM((nxs, 2, rows, rest), F32),
-            pltpu.VMEM((nx, rows, rest), F32),
+            pltpu.VMEM((nx, nz, rows, low), BF16),
+            pltpu.VMEM((nz, rows, low), F32),
+            pltpu.VMEM((2, rows, low), F32),
+            pltpu.VMEM((nz - 1, rows, low), F32),
+            pltpu.VMEM((chunks, 2, per, 2, rows, high), BF16),
+            pltpu.VMEM((chunks, nz - 1, per, 2, rows, high), BF16),
+            pltpu.VMEM((nxs, 2, rows, high), F32),
+            pltpu.VMEM((nx, rows, high), F32),
             pltpu.SemaphoreType.DMA((N_SEMS,)),
             pltpu.SemaphoreType.DMA((N_SEMS,)),
             pltpu.SemaphoreType.DMA((64,)),

time: 71.9 us -> 72.8 us (1.013)
  no operation moved by 1% of the time
where the time goes in v11:
time: 72.8 us; the launch traced here: 72.4 us
  Pallas kernels  71.8 us (99%)
    pallas_call x1, Pallas kernels, body(): pl.pallas_call(functools.partial(kernel, nz, ny, chunks), out_shape=(pltp...  70.3 us

profile of v11, /device:TPU:1, one launch (start us, length us, event | category | flops | bytes accessed | tf_op | source)
XLA Modules:
  0.0 72.4 jit_solution(15641059419132870467)
XLA Ops:
  0.6 70.3 %shard_map.84 = (bf16[16,768]{1,0:T(8,128)(2,1)S(1)}, bf16[768,768]{1,0:T(8,128)(2,1)S(1)}, bf16[768,768]{1,0:T(8,128)(2,1)S(1)}, f32[768]{0:T(1024)S(1)}) custom-call(bf16[16,768]{1,0:T(8,128)(2,1)} %tokens.1, bf16[768,768]{1,0:T(8,128)(2,1)} %weight_in.1, f32[768]{0:T(1024)} %bias_in.1, bf16[768,768]{1,0:T(8,128)(2,1)} %weight_out.1, bf16[16,768]{1,0:T(8,128)(2,1)} %out_grad.1), custom_call_target="tpu_custom_call" | custom-call | tf_op jit(solution)/shard_map/pallas_call | solution.py:642
  71.0 1.4 %shard_map.85 = (bf16[16,768]{1,0:T(8,128)(2,1)}, bf16[768,768]{1,0:T(8,128)(2,1)}, bf16[768,768]{1,0:T(8,128)(2,1)}, f32[768]{0:T(1024)}) custom-call(bf16[16,768]{1,0:T(8,128)(2,1)S(1)} %get-tuple-element.8.refs_0_, bf16[768,768]{1,0:T(8,128)(2,1)S(1)} %get-tuple-element.9.refs_1_, bf16[768,768]{1,0:T(8,128)(2,1)S(1)} %get-tuple-element.10.refs_2_, ...), custom_call_target="tpu_custom_call" | custom-call | tf_op jit(solution)/shard_map/pallas_call | solution.py:684
